TPU v7x, 32 devices: a whole 2x2x4 slice. The times are simulated.
32 devices in a mesh: outer: 4 (over z), inner: 8 (over y, x, core).
Axes of the slice: x: 2, y: 2, z: 4, core: 2. Of those that a mesh axis runs over, the one named last changes fastest.
Arguments:
- observed: float32 [32768, 768], P(('outer', 'inner')), may hold values from -6 to 6
- leaf_order: int32 [32, 1024], P(('outer', 'inner')), may hold values from 0 to 1023, each once within a row
- leaf_inverse: bfloat16 [32768, 1024], P(('outer', 'inner')), may hold values from -0.1875 to 0.1875
- project_basis: bfloat16 [32768, 640], P(('outer', 'inner')), may hold values from -0.1875 to 0.1875
- correct_basis: bfloat16 [32768, 640], P(('outer', 'inner')), may hold values from -0.375 to 0.375
- coupling: bfloat16 [8192, 256], P(('outer', 'inner'))
- trend_basis: bfloat16 [32768, 256], P(('outer', 'inner')), may hold values from -0.1875 to 0.1875
- trend_correct: bfloat16 [32768, 256], P(('outer', 'inner')), may hold values from -0.375 to 0.375
Outputs:
- solution: float32 [32768, 768], P(('outer', 'inner'))
All inputs are finite; a program needn't handle non-finite values.
Results may differ from a plain program's by a relative error of at most 0.013.
Values may be sent and summed in bfloat16 or wider, within the bound.
A program may use at most 64 MiB of HBM per device.

v0:
```python
import jax
import jax.numpy as jnp
from jax import lax
from jax.sharding import PartitionSpec as P


def from_partner(value, axis, distance):
    mask = 2**distance
    pairs = [(source, source ^ mask) for source in range(lax.axis_size(axis))]
    return lax.ppermute(value, axis, pairs)


def child_partner(subtotal, bit_no, bits_inner):
    if bit_no < bits_inner:
        return from_partner(subtotal, "inner", bit_no)
    return from_partner(subtotal.astype(jnp.bfloat16), "outer", bit_no - bits_inner).astype(
        subtotal.dtype
    )


def sibling_of(subtotal, bit_no, bits_inner):
    if bit_no < bits_inner:
        return from_partner(subtotal, "inner", bit_no)
    return from_partner(subtotal.astype(jnp.bfloat16), "outer", bit_no - bits_inner).astype(
        subtotal.dtype
    )


def body(
    observed,
    leaf_order,
    leaf_inverse,
    project_basis,
    correct_basis,
    coupling,
    trend_basis,
    trend_correct,
):
    bits_inner = lax.axis_size("inner").bit_length() - 1
    bits_outer = lax.axis_size("outer").bit_length() - 1
    levels_all = bits_inner + bits_outer
    rank = correct_basis.shape[1] // levels_all
    pos_inner = lax.axis_index("inner")
    pos_outer = lax.axis_index("outer")
    highest = lax.Precision.HIGHEST
    ordered = jnp.take(observed, leaf_order[0], axis=0).astype(jnp.bfloat16)
    estimate = jnp.dot(leaf_inverse, ordered, preferred_element_type=jnp.float32)
    group_slots = lax.all_gather(coupling, "inner", axis=0, tiled=True)
    head_slot = lax.slice_in_dim(group_slots, 0, 2 * rank, axis=0)
    outer_slots = lax.all_gather(head_slot, "outer", axis=0, tiled=True)
    contract = (((0,), (0,)), ((), ()))
    for level_no in range(1, levels_all + 1):
        child_bits = level_no - 1
        estimate_bf = estimate.astype(jnp.bfloat16)
        basis = project_basis[:, child_bits * rank : level_no * rank]
        partial_value = lax.dot_general(
            basis, estimate_bf, contract, preferred_element_type=jnp.float32
        )
        if child_bits < bits_inner:
            span = 1 << child_bits
            side_bit = pos_inner // span % 2
            owner = pos_inner // (2 * span) * (2 * span) + span
            slots = group_slots
        else:
            span = 1 << child_bits - bits_inner
            side_bit = pos_outer // span % 2
            owner = pos_outer // (2 * span) * (2 * span) + span
            slots = outer_slots
        subtotal, start_bit = (partial_value, 0)
        for bit_no in range(start_bit, child_bits):
            subtotal = subtotal + child_partner(subtotal, bit_no, bits_inner)
        sibling = sibling_of(subtotal, child_bits, bits_inner)
        own_rows = lax.dynamic_slice_in_dim(slots, (owner * 2 + side_bit) * rank, rank, 0)
        first_half = jnp.where(side_bit == 0, subtotal, sibling)
        second_half = jnp.where(side_bit == 0, sibling, subtotal)
        stacked = jnp.concatenate([first_half, second_half], 0)
        factor = jnp.dot(
            own_rows.astype(jnp.float32),
            stacked,
            precision=highest,
            preferred_element_type=jnp.float32,
        ).astype(jnp.bfloat16)
        columns = correct_basis[:, child_bits * rank : level_no * rank]
        estimate = estimate - jnp.dot(columns, factor, preferred_element_type=jnp.float32)
    trend_part = lax.dot_general(
        trend_basis, estimate.astype(jnp.bfloat16), contract, preferred_element_type=jnp.float32
    )
    trend_sum = lax.psum(trend_part, ("outer", "inner"))
    trend_block = lax.slice_in_dim(outer_slots, 0, 2 * rank, axis=0)
    trend_factor = jnp.dot(
        trend_block, trend_sum.astype(jnp.bfloat16), preferred_element_type=jnp.float32
    ).astype(jnp.bfloat16)
    return estimate - jnp.dot(trend_correct, trend_factor, preferred_element_type=jnp.float32)


def solution(mesh):
    placed = (
        P(("outer", "inner"), None),
        P(("outer", "inner"), None),
        P(("outer", "inner"), None),
        P(("outer", "inner"), None),
        P(("outer", "inner"), None),
        P(("outer", "inner"), None),
        P(("outer", "inner"), None),
        P(("outer", "inner"), None),
    )
    return jax.shard_map(
        body, mesh=mesh, in_specs=placed, out_specs=P(("outer", "inner"), None), check_vma=False
    )
```

profile of v0, /device:TPU:1, one launch (start us, length us, event | category | flops | bytes accessed | tf_op | source)
XLA Modules:
  0.0 245.3 jit_solution(10457475349602870045)
XLA Ops:
  8.4 5.0 %gather_fusion = bf16[1024,768]{1,0:T(8,128)(2,1)} fusion(f32[1024,768]{1,0:T(8,128)S(1)} %copy-done, s32[1024]{0:T(1024)S(1)} %broadcast_clamp_fusion), kind=kCustom, calls=%fused_computation | custom fusion | bytes 3149824 | tf_op jit(solution)/shard_map/jit(_take)/gather | solution.py:46
  13.4 4.2 %fusion = f32[768,1024]{1,0:T(8,128)S(1)} fusion(bf16[1024,1024]{1,0:T(8,128)(2,1)} %param.10, bf16[1024,768]{1,0:T(8,128)(2,1)} %gather_fusion, pred[1024]{0:T(1024)(128)(4,1)S(1)} %compare_and_fusion), kind=kOutput, calls=%fused_computation.8 | convolution fusion | flops 1611399168 | bytes 6816768 | tf_op jit(solution)/shard_map/dot_general | solution.py:47
  17.7 1.7 copy-done.7
  19.3 1.6 fusion.18
  21.1 1.8 collective-permute-done
  22.9 1.9 broadcast_select_fusion.5
  24.8 10.5 %all-gather.2.cloned.1.call-done = bf16[2048,256]{1,0:T(8,128)(2,1)} async-done(((bf16[256,256]{1,0:T(8,128)(2,1)}), bf16[2048,256]{1,0:T(8,128)(2,1)}) %all-gather.2.cloned.1.call-update) | async-done | bytes 1048592 | tf_op jit(solution)/shard_map/all_gather | solution.py:48
  35.3 1.6 convolution_convert_fusion.5
  36.9 2.6 %convolution_subtract_fusion.4 = f32[768,1024]{1,0:T(8,128)S(1)} fusion(f32[768,1024]{1,0:T(8,128)} %copy-done.7, bf16[128,768]{1,0:T(8,128)(2,1)S(1)} %convolution_convert_fusion.5, bf16[1024,640]{1,0:T(8,128)(2,1)} %param.12), kind=kOutput, calls=%fused_computation.7 | convolution fusion | flops 202113024 | bytes 6750208 | tf_op jit(solution)/shard_map/dot_general | solution.py:84
  39.5 1.8 fusion.21
  41.6 1.5 collective-permute-done.1
  43.2 1.3 collective-permute-start.2
  44.4 9.4 %collective-permute-done.2 = f32[128,768]{1,0:T(8,128)} collective-permute-done((f32[128,768]{1,0:T(8,128)S(1)}, f32[128,768]{1,0:T(8,128)}, u32[]{:S(2)}, u32[]{:S(2)}) %collective-permute-start.2) | collective-permute-done | bytes 393248 | tf_op jit(solution)/shard_map/ppermute | solution.py:10
  54.9 1.3 convolution_convert_fusion.4
  56.1 2.6 %convolution_subtract_fusion.3 = f32[768,1024]{1,0:T(8,128)S(1)} fusion(f32[768,1024]{1,0:T(8,128)} %copy-done.6, bf16[128,768]{1,0:T(8,128)(2,1)S(1)} %convolution_convert_fusion.4, bf16[1024,640]{1,0:T(8,128)(2,1)} %param.12), kind=kOutput, calls=%fused_computation.6 | convolution fusion | flops 202113024 | bytes 6750208 | tf_op jit(solution)/shard_map/dot_general | solution.py:84
  58.8 1.8 fusion.24
  61.7 1.3 collective-permute-done.3
  63.1 1.3 collective-permute-start.4
  64.4 9.1 %collective-permute-done.4 = f32[128,768]{1,0:T(8,128)S(1)} collective-permute-done((f32[128,768]{1,0:T(8,128)S(1)}, f32[128,768]{1,0:T(8,128)S(1)}, u32[]{:S(2)}, u32[]{:S(2)}) %collective-permute-start.4) | collective-permute-done | bytes 393248 | tf_op jit(solution)/shard_map/ppermute | solution.py:10
  73.6 1.2 collective-permute-start.5
  74.8 8.4 %collective-permute-done.5 = f32[128,768]{1,0:T(8,128)} collective-permute-done((f32[128,768]{1,0:T(8,128)S(1)}, f32[128,768]{1,0:T(8,128)}, u32[]{:S(2)}, u32[]{:S(2)}) %collective-permute-start.5) | collective-permute-done | bytes 393248 | tf_op jit(solution)/shard_map/ppermute | solution.py:10
  84.2 1.3 convolution_convert_fusion.3
  85.5 2.6 %convolution_subtract_fusion.2 = f32[768,1024]{1,0:T(8,128)S(1)} fusion(f32[768,1024]{1,0:T(8,128)} %copy-done.5, bf16[128,768]{1,0:T(8,128)(2,1)S(1)} %convolution_convert_fusion.3, bf16[1024,640]{1,0:T(8,128)(2,1)} %param.12), kind=kOutput, calls=%fused_computation.5 | convolution fusion | flops 202113024 | bytes 6750208 | tf_op jit(solution)/shard_map/dot_general | solution.py:84
  88.1 1.8 fusion.27
  90.0 2.2 collective-permute-start.6
  92.1 1.3 collective-permute-done.6
  93.6 1.2 collective-permute-start.7
  94.8 9.1 %collective-permute-done.7 = f32[128,768]{1,0:T(8,128)S(1)} collective-permute-done((f32[128,768]{1,0:T(8,128)S(1)}, f32[128,768]{1,0:T(8,128)S(1)}, u32[]{:S(2)}, u32[]{:S(2)}) %collective-permute-start.7) | collective-permute-done | bytes 393248 | tf_op jit(solution)/shard_map/ppermute | solution.py:10
  106.1 7.5 %collective-permute-done.8 = f32[128,768]{1,0:T(8,128)} collective-permute-done((f32[128,768]{1,0:T(8,128)S(1)}, f32[128,768]{1,0:T(8,128)}, u32[]{:S(2)}, u32[]{:S(2)}) %collective-permute-start.8) | collective-permute-done | bytes 393248 | tf_op jit(solution)/shard_map/ppermute | solution.py:10
  114.6 1.3 collective-permute-start.9
  115.9 14.6 %all_gather.7 = bf16[1024,256]{1,0:T(8,128)(2,1)S(1)} all-gather(bf16[256,256]{1,0:T(8,128)(2,1)S(1)} %slice.50), channel_id=1, replica_groups=mesh['outer'=4,'inner'=8] {'outer'}, dimensions={0}, use_global_device_ids=true | all-gather | bytes 655360 | tf_op jit(solution)/shard_map/all_gather | solution.py:50
  131.7 1.6 convolution_subtract_fusion.1
  133.3 1.8 fusion.30
  135.1 4.6 %collective-permute-start.10 = (f32[128,768]{1,0:T(8,128)S(1)}, f32[128,768]{1,0:T(8,128)S(1)}, u32[]{:S(2)}, u32[]{:S(2)}) collective-permute-start(f32[128,768]{1,0:T(8,128)S(1)} %fusion.30), channel_id=1, source_target_pairs={{0,1},{1,0},{2,3},{3,2},{4,5},{5,4},{6,7},{7,6},{8,9},{9,8},{10,11... | collective-permute-start | bytes 1179656 | tf_op jit(solution)/shard_map/ppermute | solution.py:10
  139.7 1.3 collective-permute-done.10
  141.1 1.3 collective-permute-start.11
  142.4 9.1 %collective-permute-done.11 = f32[128,768]{1,0:T(8,128)S(1)} collective-permute-done((f32[128,768]{1,0:T(8,128)S(1)}, f32[128,768]{1,0:T(8,128)S(1)}, u32[]{:S(2)}, u32[]{:S(2)}) %collective-permute-start.11) | collective-permute-done | bytes 393248 | tf_op jit(solution)/shard_map/ppermute | solution.py:10
  151.5 1.3 collective-permute-start.12
  152.8 8.2 %collective-permute-done.12 = f32[128,768]{1,0:T(8,128)S(1)} collective-permute-done((f32[128,768]{1,0:T(8,128)S(1)}, f32[128,768]{1,0:T(8,128)S(1)}, u32[]{:S(2)}, u32[]{:S(2)}) %collective-permute-start.12) | collective-permute-done | bytes 393248 | tf_op jit(solution)/shard_map/ppermute | solution.py:10
  161.4 4.2 %collective-permute-done.13 = bf16[128,768]{1,0:T(8,128)(2,1)S(1)} collective-permute-done((bf16[128,768]{1,0:T(8,128)(2,1)S(1)}, bf16[128,768]{1,0:T(8,128)(2,1)S(1)}, u32[]{:S(2)}, u32[]{:S(2)}) %collective-permute-start.13) | collective-permute-done | bytes 196640 | tf_op jit(solution)/shard_map/ppermute | solution.py:10
  168.1 9.6 %collective-permute-done.14 = bf16[128,768]{1,0:T(8,128)(2,1)} collective-permute-done((bf16[128,768]{1,0:T(8,128)(2,1)}, bf16[128,768]{1,0:T(8,128)(2,1)}, u32[]{:S(2)}, u32[]{:S(2)}) %collective-permute-start.14) | collective-permute-done | bytes 196640 | tf_op jit(solution)/shard_map/ppermute | solution.py:10
  178.8 1.3 convolution_convert_fusion.1
  180.1 2.6 %convolution_subtract_fusion = f32[768,1024]{1,0:T(8,128)S(1)} fusion(f32[768,1024]{1,0:T(8,128)} %copy-done.2, bf16[128,768]{1,0:T(8,128)(2,1)S(1)} %convolution_convert_fusion.1, bf16[1024,640]{1,0:T(8,128)(2,1)} %param.12), kind=kOutput, calls=%fused_computation.3 | convolution fusion | flops 202113024 | bytes 6750208 | tf_op jit(solution)/shard_map/dot_general | solution.py:84
  182.7 1.7 copy-done.1
  184.4 1.5 fusion.15
  185.9 44.6 %all-reduce.1 = bf16[256,768]{0,1:T(8,128)(2,1)S(1)} all-reduce(f32[256,768]{0,1:T(8,128)} %fusion.15), channel_id=1, replica_groups=mesh['outer'=4,'inner'=8] {'outer','inner'}, use_global_device_ids=true, to_apply=%region_0.1 | all-reduce | flops 196608 | bytes 1179648 | tf_op jit(solution)/shard_map/psum | solution.py:88
  230.5 4.5 %subtract_bitcast_fusion = f32[1024,768]{0,1:T(8,128)} fusion(f32[768,1024]{1,0:T(8,128)} %copy-done.1, bf16[1024,256]{1,0:T(8,128)(2,1)} %param.15, bf16[256,768]{0,1:T(8,128)(2,1)S(1)} %all-reduce.1, bf16[1024,256]{1,0:T(8,128)(2,1)} %copy-done.8), kind=kOutput, calls=%fused_computation.1 | convolution fusion | flops 504299520 | bytes 7340032 | tf_op jit(solution)/shard_map/dot_general | solution.py:93
  234.9 3.5 %copy.10 = f32[1024,768]{1,0:T(8,128)} copy(f32[1024,768]{0,1:T(8,128)} %subtract_bitcast_fusion) | data formatting | bytes 6291456 | tf_op jit(solution)/shard_map/sub | solution.py:93
  (50 shorter events, 14.2 us)
Async XLA Ops:
  6.5 1.9 copy-start
  6.5 28.8 %all-gather.2.cloned.1.call-start = ((), (), s32[]{:S(2)}) async-start(), calls=%async_computation | async-start | bytes 1179648 | tf_op jit(solution)/shard_map/all_gather | solution.py:48
  8.4 5.0 %copy-start.11 = (s32[1,1024]{1,0:T(1,128)S(1)}, s32[1,1024]{1,0:T(1,128)}, u32[]{:S(2)}) copy-start(s32[1,1024]{1,0:T(1,128)} %param.9) | copy-start | bytes 12292
  17.6 1.7 copy-start.7
  20.9 1.9 collective-permute-start
  39.5 3.7 %copy-start.6 = (f32[768,1024]{1,0:T(8,128)}, f32[768,1024]{1,0:T(8,128)S(1)}, u32[]{:S(2)}) copy-start(f32[768,1024]{1,0:T(8,128)S(1)} %convolution_subtract_fusion.4) | copy-start | bytes 9437188
  41.3 1.8 collective-permute-start.1
  43.2 10.6 %collective-permute-start.2 = (f32[128,768]{1,0:T(8,128)S(1)}, f32[128,768]{1,0:T(8,128)}, u32[]{:S(2)}, u32[]{:S(2)}) collective-permute-start(f32[128,768]{1,0:T(8,128)S(1)} %add.133), channel_id=1, source_target_pairs={{0,2},{1,3},{2,0},{3,1},{4,6},{5,7},{6,4},{7,5},{8,10},{9,11},{10,... | collective-permute-start | bytes 1179656 | tf_op jit(solution)/shard_map/ppermute | solution.py:10
  58.8 4.4 %copy-start.5 = (f32[768,1024]{1,0:T(8,128)}, f32[768,1024]{1,0:T(8,128)S(1)}, u32[]{:S(2)}) copy-start(f32[768,1024]{1,0:T(8,128)S(1)} %convolution_subtract_fusion.3) | copy-start | bytes 9437188
  60.6 2.5 %collective-permute-start.3 = (f32[128,768]{1,0:T(8,128)S(1)}, f32[128,768]{1,0:T(8,128)S(1)}, u32[]{:S(2)}, u32[]{:S(2)}) collective-permute-start(f32[128,768]{1,0:T(8,128)S(1)} %fusion.24), channel_id=1, source_target_pairs={{0,1},{1,0},{2,3},{3,2},{4,5},{5,4},{6,7},{7,6},{8,9},{9,8},{10,11... | collective-permute-start | bytes 1179656 | tf_op jit(solution)/shard_map/ppermute | solution.py:10
  63.1 10.4 %collective-permute-start.4 = (f32[128,768]{1,0:T(8,128)S(1)}, f32[128,768]{1,0:T(8,128)S(1)}, u32[]{:S(2)}, u32[]{:S(2)}) collective-permute-start(f32[128,768]{1,0:T(8,128)S(1)} %add.138), channel_id=1, source_target_pairs={{0,2},{1,3},{2,0},{3,1},{4,6},{5,7},{6,4},{7,5},{8,10},{9,11},{10,... | collective-permute-start | bytes 1179656 | tf_op jit(solution)/shard_map/ppermute | solution.py:10
  73.6 9.6 %collective-permute-start.5 = (f32[128,768]{1,0:T(8,128)S(1)}, f32[128,768]{1,0:T(8,128)}, u32[]{:S(2)}, u32[]{:S(2)}) collective-permute-start(f32[128,768]{1,0:T(8,128)S(1)} %add.139), channel_id=1, source_target_pairs={{0,4},{1,5},{2,6},{3,7},{4,0},{5,1},{6,2},{7,3},{8,12},{9,13},{10,... | collective-permute-start | bytes 1179656 | tf_op jit(solution)/shard_map/ppermute | solution.py:10
  88.1 5.5 %copy-start.3 = (f32[768,1024]{1,0:T(8,128)}, f32[768,1024]{1,0:T(8,128)S(1)}, u32[]{:S(2)}) copy-start(f32[768,1024]{1,0:T(8,128)S(1)} %convolution_subtract_fusion.2) | copy-start | bytes 9437188
  90.0 3.5 %collective-permute-start.6 = (f32[128,768]{1,0:T(8,128)S(1)}, f32[128,768]{1,0:T(8,128)S(1)}, u32[]{:S(2)}, u32[]{:S(2)}) collective-permute-start(f32[128,768]{1,0:T(8,128)S(1)} %fusion.27), channel_id=1, source_target_pairs={{0,1},{1,0},{2,3},{3,2},{4,5},{5,4},{6,7},{7,6},{8,9},{9,8},{10,11... | collective-permute-start | bytes 1179656 | tf_op jit(solution)/shard_map/ppermute | solution.py:10
  93.6 10.4 %collective-permute-start.7 = (f32[128,768]{1,0:T(8,128)S(1)}, f32[128,768]{1,0:T(8,128)S(1)}, u32[]{:S(2)}, u32[]{:S(2)}) collective-permute-start(f32[128,768]{1,0:T(8,128)S(1)} %add.144), channel_id=1, source_target_pairs={{0,2},{1,3},{2,0},{3,1},{4,6},{5,7},{6,4},{7,5},{8,10},{9,11},{10,... | collective-permute-start | bytes 1179656 | tf_op jit(solution)/shard_map/ppermute | solution.py:10
  104.0 9.6 %collective-permute-start.8 = (f32[128,768]{1,0:T(8,128)S(1)}, f32[128,768]{1,0:T(8,128)}, u32[]{:S(2)}, u32[]{:S(2)}) collective-permute-start(f32[128,768]{1,0:T(8,128)S(1)} %add.145), channel_id=1, source_target_pairs={{0,4},{1,5},{2,6},{3,7},{4,0},{5,1},{6,2},{7,3},{8,12},{9,13},{10,... | collective-permute-start | bytes 1179656 | tf_op jit(solution)/shard_map/ppermute | solution.py:10
  106.1 25.6 %copy-start.4 = (f32[768,1024]{1,0:T(8,128)S(1)}, f32[768,1024]{1,0:T(8,128)}, u32[]{:S(2)}) copy-start(f32[768,1024]{1,0:T(8,128)} %copy-done.3) | copy-start | bytes 9437188
  114.6 15.9 %collective-permute-start.9 = (bf16[128,768]{1,0:T(8,128)(2,1)S(1)}, bf16[128,768]{1,0:T(8,128)(2,1)S(1)}, u32[]{:S(2)}, u32[]{:S(2)}) collective-permute-start(bf16[128,768]{1,0:T(8,128)(2,1)S(1)} %get-tuple-element.7), channel_id=1, source_target_pairs={{0,8},{8,0},{16,24},{24,16},{1,9},{9,1},{17,25},{25,17},{2,10},{10... | collective-permute-start | bytes 589832 | tf_op jit(solution)/shard_map/ppermute | solution.py:10
  130.5 0.8 copy-start.8
  133.3 7.8 %copy-start.2 = (f32[768,1024]{1,0:T(8,128)}, f32[768,1024]{1,0:T(8,128)S(1)}, u32[]{:S(2)}) copy-start(f32[768,1024]{1,0:T(8,128)S(1)} %convolution_subtract_fusion.1) | copy-start | bytes 9437188
  135.1 5.9 %collective-permute-start.10 = (f32[128,768]{1,0:T(8,128)S(1)}, f32[128,768]{1,0:T(8,128)S(1)}, u32[]{:S(2)}, u32[]{:S(2)}) collective-permute-start(f32[128,768]{1,0:T(8,128)S(1)} %fusion.30), channel_id=1, source_target_pairs={{0,1},{1,0},{2,3},{3,2},{4,5},{5,4},{6,7},{7,6},{8,9},{9,8},{10,11... | collective-permute-start | bytes 1179656 | tf_op jit(solution)/shard_map/ppermute | solution.py:10
  141.1 10.4 %collective-permute-start.11 = (f32[128,768]{1,0:T(8,128)S(1)}, f32[128,768]{1,0:T(8,128)S(1)}, u32[]{:S(2)}, u32[]{:S(2)}) collective-permute-start(f32[128,768]{1,0:T(8,128)S(1)} %add.151), channel_id=1, source_target_pairs={{0,2},{1,3},{2,0},{3,1},{4,6},{5,7},{6,4},{7,5},{8,10},{9,11},{10,... | collective-permute-start | bytes 1179656 | tf_op jit(solution)/shard_map/ppermute | solution.py:10
  151.5 9.5 %collective-permute-start.12 = (f32[128,768]{1,0:T(8,128)S(1)}, f32[128,768]{1,0:T(8,128)S(1)}, u32[]{:S(2)}, u32[]{:S(2)}) collective-permute-start(f32[128,768]{1,0:T(8,128)S(1)} %add.152), channel_id=1, source_target_pairs={{0,4},{1,5},{2,6},{3,7},{4,0},{5,1},{6,2},{7,3},{8,12},{9,13},{10,... | collective-permute-start | bytes 1179656 | tf_op jit(solution)/shard_map/ppermute | solution.py:10
  161.1 4.6 %collective-permute-start.13 = (bf16[128,768]{1,0:T(8,128)(2,1)S(1)}, bf16[128,768]{1,0:T(8,128)(2,1)S(1)}, u32[]{:S(2)}, u32[]{:S(2)}) collective-permute-start(bf16[128,768]{1,0:T(8,128)(2,1)S(1)} %get-tuple-element.5), channel_id=1, source_target_pairs={{0,8},{8,0},{16,24},{24,16},{1,9},{9,1},{17,25},{25,17},{2,10},{10... | collective-permute-start | bytes 589832 | tf_op jit(solution)/shard_map/ppermute | solution.py:10
  165.7 0.7 copy-start.9
  167.1 10.6 %collective-permute-start.14 = (bf16[128,768]{1,0:T(8,128)(2,1)}, bf16[128,768]{1,0:T(8,128)(2,1)}, u32[]{:S(2)}, u32[]{:S(2)}) collective-permute-start(bf16[128,768]{1,0:T(8,128)(2,1)} %fusion.60), channel_id=1, source_target_pairs={{0,16},{8,24},{16,0},{24,8},{1,17},{9,25},{17,1},{25,9},{2,18},{10... | collective-permute-start | bytes 589832 | tf_op jit(solution)/shard_map/ppermute | solution.py:10
  180.1 4.3 %copy-start.10 = (bf16[1024,256]{1,0:T(8,128)(2,1)S(1)}, bf16[1024,256]{1,0:T(8,128)(2,1)}, u32[]{:S(2)}) copy-start(bf16[1024,256]{1,0:T(8,128)(2,1)} %param.14) | copy-start | bytes 1572868
  182.7 1.7 copy-start.1
Sparse Core Ops, SparseCore 0:
  9.2 25.9 all-gather.1
where the time goes:
time: 248 us; the launch traced here: 245 us
  waiting for transfers between devices  93.2 us (38%)
  blocking collectives  59.2 us (24%)
  matrix products  36.9 us (15%)
  starting transfers between devices  19.6 us (8%)
  local copies, waits for them, and re-layouts  14.5 us (6%)
  between operations  13.7 us (6%)
  other arithmetic  8.26 us (3%)
    ppermute x15, waiting for transfers between devices, from_partner(): return lax.ppermute(value, axis, pairs)  82 us
    psum x1, blocking collectives, body(): trend_sum = lax.psum(trend_part, ('outer', 'inner'))  44.6 us
    ppermute x15, starting transfers between devices, from_partner(): return lax.ppermute(value, axis, pairs)  19.6 us
    all_gather x1, blocking collectives, body(): outer_slots = lax.all_gather(head_slot, 'outer', axis=0, tiled=True)  14.6 us
    dot_general x5, matrix products, body(): jnp.dot(columns, factor, preferred_element_type=jnp.float32)  12 us
    all_gather x1, waiting for transfers between devices, body(): group_slots = lax.all_gather(coupling, 'inner', axis=0, tiled=True)  10.5 us
    dot_general x5, matrix products, body(): lax.dot_general(basis, estimate_bf, contract, preferred_element_type=jnp....  8.96 us
    dot_general x5, matrix products, body(): jnp.dot(own_rows.astype(jnp.float32), stacked, precision=highest, preferr...  5.78 us
  transfers between devices with their start and end apart: 16, of which 15 were waited for; matrix products, arithmetic and copies ran while one was open for 6% of the time, Pallas kernels for 0%

commit v1 on v0

v1 whole, which is shorter than its diff:
```python
import functools

import jax
import jax.numpy as jnp
from jax import lax
from jax.experimental import pallas as pl
from jax.experimental.pallas import tpu as pltpu
from jax.sharding import PartitionSpec as P

MESH = pl.DeviceIdType.MESH
BF = jnp.bfloat16
F32 = jnp.float32
NT = (((1,), (1,)), ((), ()))


def dot(a, b):
    return jnp.dot(a, b, preferred_element_type=F32)


def dot_nt(a, b):
    return lax.dot_general(a, b, NT, preferred_element_type=F32)


def plan(cols, levels, rank, trend):
    held, part = [], []
    now = cols
    for _ in range(levels):
        held.append(now)
        if now % 32 == 0:
            now //= 2
        part.append(now)
    rows = [(levels - s) * rank + trend for s in range(levels + 1)]
    width = [sum(rows[s + 1 :]) for s in range(levels)]
    return held, part, rows, width


def sweep_kernel(
    bits_inner,
    levels,
    rank,
    tile,
    observed,
    order,
    inverse,
    project,
    correct,
    coupling,
    trend,
    estimate_out,
    factor_out,
    obs_v,
    obs_bf,
    order_v,
    inv_v,
    basis_v,
    correct_v,
    hot_v,
    est_v,
    est_t,
    blocks,
    factors,
    *rest,
):
    leaf, cols = observed.shape
    trend_rank = trend.shape[1]
    held, part, rows, width = plan(cols, levels, rank, trend_rank)
    sums = rest[: levels + 1]
    x_send = rest[levels + 1 : 2 * levels + 1]
    x_recv = rest[2 * levels + 1 : 3 * levels + 1]
    g_send = rest[3 * levels + 1 : 4 * levels + 1]
    g_recv = rest[4 * levels + 1 : 5 * levels + 1]
    sib = rest[5 * levels + 1 : 6 * levels + 1]
    local_sem, send_sem, recv_sem = rest[6 * levels + 1 :]

    outer, inner = lax.axis_index("outer"), lax.axis_index("inner")
    bits, partners = [], []
    for s in range(levels):
        if s < bits_inner:
            span = 1 << s
            bit = lax.rem(inner // span, 2)
            partners.append((outer, inner + (1 - 2 * bit) * span))
        else:
            span = 1 << (s - bits_inner)
            bit = lax.rem(outer // span, 2)
            partners.append((outer + (1 - 2 * bit) * span, inner))
        bits.append(bit)

    def local(src, dst, i):
        copy = pltpu.make_async_copy(src, dst, local_sem.at[i])
        copy.start()
        return copy

    wide = levels * rank
    c_block = local(coupling, blocks.at[0], 0)
    c_correct = local(correct, correct_v, 1)
    c_project = local(project, basis_v.at[:, pl.ds(0, wide)], 2)
    c_trend = local(trend, basis_v.at[:, pl.ds(wide, trend_rank)], 3)
    c_order = local(order, order_v, 4)
    c_inv = local(inverse, inv_v, 5)
    c_obs = local(observed, obs_v, 6)

    barrier = pltpu.get_barrier_semaphore()
    for partner in partners:
        pl.semaphore_signal(barrier, inc=1, device_id=partner, device_id_type=MESH)
    pl.semaphore_wait(barrier, levels)

    def remote(src, dst, kind, s):
        copy = pltpu.make_async_remote_copy(
            src_ref=src,
            dst_ref=dst,
            send_sem=send_sem.at[kind, s],
            recv_sem=recv_sem.at[kind, s],
            device_id=partners[s],
            device_id_type=MESH,
        )
        copy.start()
        return copy

    flying = []
    block_copies, gram_copies, x_copies, sib_copies = {}, {}, {}, {}
    pending = jnp.int32(0)
    block_of = []

    def send_block(s):
        block_copies[s] = remote(blocks.at[pending], blocks.at[s + 1], 0, s)

    def send_gram(s):
        gram_copies[s] = remote(g_send[s], g_recv[s], 1, s)

    def send_x(s):
        x_copies[s] = remote(x_send[s], x_recv[s], 2, s)

    def finish_small(s):
        nonlocal pending
        block_copies[s].wait_recv()
        block_of.append(jnp.where(bits[s] == 1, pending, s + 1))
        pending = jnp.where(bits[s] == 1, s + 1, pending)
        if s + 1 < levels:
            send_block(s + 1)
        gram_copies[s].wait_recv()
        if s + 1 < levels:
            skip = rows[s + 1]
            g_send[s + 1][...] = (
                g_send[s][:, skip:].astype(F32) + g_recv[s][:, skip:].astype(F32)
            ).astype(BF)
            send_gram(s + 1)

    c_block.wait()
    send_block(0)

    c_correct.wait()
    c_project.wait()
    c_trend.wait()
    at = 0
    for s in range(levels):
        columns_t = correct_v[:, s * rank : (s + 1) * rank].T
        g_send[0][:, at : at + rows[s + 1]] = dot(
            columns_t, basis_v[:, (s + 1) * rank :]
        ).astype(BF)
        at += rows[s + 1]
    send_gram(0)

    c_order.wait()
    steps = leaf // tile

    def make_hot(t, carry):
        r0 = pl.multiple_of(t * tile, tile)
        ids = lax.broadcasted_iota(jnp.int32, (tile, leaf), 0) + r0
        hot_v[pl.ds(r0, tile), :] = jnp.where(ids == order_v[...], 1.0, 0.0).astype(BF)
        return carry

    lax.fori_loop(0, steps, make_hot, 0)
    c_obs.wait()

    def cast(t, carry):
        r0 = pl.multiple_of(t * tile, tile)
        obs_bf[pl.ds(r0, tile), :] = obs_v[pl.ds(r0, tile), :].astype(BF)
        return carry

    lax.fori_loop(0, steps, cast, 0)
    c_inv.wait()

    def make_estimate(t, carry):
        r0 = pl.multiple_of(t * tile, tile)
        ordered_inv = dot_nt(inv_v[pl.ds(r0, tile), :], hot_v[...]).astype(BF)
        value = dot(ordered_inv, obs_bf[...])
        est_v[pl.ds(r0, tile), :] = value
        est_t[:, pl.ds(r0, tile)] = value.astype(BF).T
        return carry

    lax.fori_loop(0, steps, make_estimate, 0)
    c_est = local(est_v, estimate_out, 7)

    finish_small(0)

    half = part[0]
    ctile = half // 2

    def project_half(start, into_send):
        def step(t, carry):
            c0 = pl.multiple_of(start + t * ctile, ctile)
            value = dot(est_t[pl.ds(c0, ctile), :], basis_v[...])
            d0 = pl.multiple_of(t * ctile, ctile)
            if into_send:
                x_send[0][pl.ds(d0, ctile), :] = value.astype(BF)
            else:
                sums[0][pl.ds(d0, ctile), :] = value
            return carry

        lax.fori_loop(0, 2, step, 0)

    project_half((1 - bits[0]) * half, True)
    send_x(0)
    project_half(bits[0] * half, False)

    offsets = [jnp.int32(0)]
    for s in range(levels):
        count = part[s]
        halves = held[s] != part[s]
        first_side = bits[s] == 0
        offset = offsets[s] + (bits[s] * count if halves else 0)
        offset = pl.multiple_of(offset, count)
        offsets.append(offset)
        if s > 0:
            finish_small(s)
        if s == 0 or not halves:
            own = sums[s][...]
        else:
            own = sums[s][pl.ds(pl.multiple_of(bits[s] * count, count), count), :]
        x_copies[s].wait_recv()
        other = x_recv[s][...]
        own_head = own[:, :rank].astype(BF)
        other_head = other[:, :rank]
        one = jnp.where(first_side, own_head.astype(F32), other_head.astype(F32)).astype(BF)
        two = jnp.where(first_side, other_head.astype(F32), own_head.astype(F32)).astype(BF)
        block = blocks[block_of[s]]
        factor = dot_nt(one, block[:, :rank]) + dot_nt(two, block[:, rank:])
        mine = jnp.where(first_side, factor[:, :rank], factor[:, rank:]).astype(BF)
        theirs = jnp.where(first_side, factor[:, rank:], factor[:, :rank]).astype(BF)
        factors[pl.ds(offset, count), s * rank : (s + 1) * rank] = mine
        skip = rows[s + 1]
        new = (
            own[:, rank:]
            + other[:, rank:].astype(F32)
            - dot(mine, g_send[s][:, :skip])
            - dot(theirs, g_recv[s][:, :skip])
        )
        sums[s + 1][...] = new
        if s + 1 < levels:
            after = part[s + 1]
            if held[s + 1] != after:
                away = pl.multiple_of((1 - bits[s + 1]) * after, after)
                x_send[s + 1][...] = sums[s + 1][pl.ds(away, after), :].astype(BF)
            else:
                x_send[s + 1][...] = new.astype(BF)
            send_x(s + 1)
        if halves:
            sib[s][...] = theirs
            sib_copies[s] = remote(
                sib[s],
                factors.at[pl.ds(offset, count), pl.ds(s * rank, rank)],
                3,
                s,
            )

    trend_factor = dot_nt(sums[levels][...].astype(BF), blocks[pending]).astype(BF)
    factors[pl.ds(offsets[levels], part[levels - 1]), wide:] = trend_factor

    down = []
    for s in reversed(range(levels)):
        if s not in sib_copies:
            continue
        lanes = pl.ds((s + 1) * rank, rows[s + 1])
        place = factors.at[pl.ds(offsets[s + 1], part[s]), lanes]
        copy = remote(place, place, 4, s)
        copy.wait_recv()
        sib_copies[s].wait_recv()
        down.append(copy)

    out = local(factors, factor_out, 0)
    for group in (block_copies, gram_copies, x_copies, sib_copies):
        for copy in group.values():
            copy.wait_send()
    for copy in down:
        copy.wait_send()
    c_est.wait()
    out.wait()


def apply_kernel(wide, estimate, correct, trend, factors, out):
    out[...] = (
        estimate[...]
        - dot_nt(correct[...], factors[:, :wide])
        - dot_nt(trend[...], factors[:, wide:])
    )


def body(
    bits_inner,
    levels,
    observed,
    leaf_order,
    leaf_inverse,
    project_basis,
    correct_basis,
    coupling,
    trend_basis,
    trend_correct,
):
    leaf, cols = observed.shape
    wide = correct_basis.shape[1]
    rank = wide // levels
    trend_rank = trend_basis.shape[1]
    held, part, rows, width = plan(cols, levels, rank, trend_rank)
    tile = 256 if leaf % 256 == 0 else leaf
    vm = pltpu.VMEM
    every = range(levels)
    scratch = [
        vm((leaf, cols), F32),
        vm((leaf, cols), BF),
        vm(leaf_order.shape, jnp.int32),
        vm((leaf, leaf), BF),
        vm((leaf, wide + trend_rank), BF),
        vm((leaf, wide), BF),
        vm((leaf, leaf), BF),
        vm((leaf, cols), F32),
        vm((cols, leaf), BF),
        vm((levels + 1,) + coupling.shape, BF),
        vm((cols, wide + trend_rank), BF),
    ]
    scratch += [vm((part[0], rows[0]), F32)]
    scratch += [vm((part[s], rows[s + 1]), F32) for s in every]
    scratch += [vm((part[s], rows[s]), BF) for s in every] * 2
    scratch += [vm((rank, width[s]), BF) for s in every] * 2
    scratch += [vm((part[s], rank), BF) for s in every]
    scratch += [
        pltpu.SemaphoreType.DMA((8,)),
        pltpu.SemaphoreType.DMA((5, levels)),
        pltpu.SemaphoreType.DMA((5, levels)),
    ]
    anywhere = pl.BlockSpec(memory_space=pl.ANY)
    estimate, factors = pl.pallas_call(
        functools.partial(sweep_kernel, bits_inner, levels, rank, tile),
        out_shape=(
            jax.ShapeDtypeStruct((leaf, cols), F32),
            jax.ShapeDtypeStruct((cols, wide + trend_rank), BF),
        ),
        in_specs=[anywhere] * 7,
        out_specs=(anywhere, anywhere),
        scratch_shapes=scratch,
        compiler_params=pltpu.CompilerParams(
            collective_id=0, has_side_effects=True, vmem_limit_bytes=56 * 1024 * 1024
        ),
        name="tree_sweep",
    )(observed, leaf_order, leaf_inverse, project_basis, correct_basis, coupling, trend_basis)
    return pl.pallas_call(
        functools.partial(apply_kernel, wide),
        grid=(leaf // tile,),
        out_shape=jax.ShapeDtypeStruct((leaf, cols), F32),
        in_specs=[
            pl.BlockSpec((tile, cols), lambda i: (i, 0)),
            pl.BlockSpec((tile, wide), lambda i: (i, 0)),
            pl.BlockSpec((tile, trend_rank), lambda i: (i, 0)),
            pl.BlockSpec((cols, wide + trend_rank), lambda i: (0, 0)),
        ],
        out_specs=pl.BlockSpec((tile, cols), lambda i: (i, 0)),
        compiler_params=pltpu.CompilerParams(vmem_limit_bytes=40 * 1024 * 1024),
        name="apply_factors",
    )(estimate, correct_basis, trend_correct, factors)


def solution(mesh):
    bits_inner = mesh.shape["inner"].bit_length() - 1
    bits_outer = mesh.shape["outer"].bit_length() - 1
    rows = P(("outer", "inner"), None)
    return jax.shard_map(
        functools.partial(body, bits_inner, bits_inner + bits_outer),
        mesh=mesh,
        in_specs=(rows,) * 8,
        out_specs=rows,
        check_vma=False,
    )
```

time: 248 us -> 71.9 us (0.29)
  waiting for transfers between devices: 93.2 us -> 0 us
  Pallas kernels: 0 us -> 68 us
  blocking collectives: 59.2 us -> 0 us
  matrix products: 36.9 us -> 0 us
  starting transfers between devices: 19.6 us -> 0 us
  between operations: 13.7 us -> 0.04 us
  local copies, waits for them, and re-layouts: 14.5 us -> 3.23 us
  other arithmetic: 8.26 us -> 0 us
    ppermute x15 -> x0, waiting for transfers between devices: 82 us -> none  [from_partner(): return lax.ppermute(value, axis, pairs)]
    pallas_call x0 -> x2, Pallas kernels: none -> 68 us  [the longest x1 64.4 us: body(): pl.pallas_call(functools.partial(sweep_kernel, bits_inner, levels, rank,...]
    psum x1 -> x0, blocking collectives: 44.6 us -> none  [body(): trend_sum = lax.psum(trend_part, ('outer', 'inner'))]
    dot_general x18 -> x0, matrix products: 36.9 us -> none  [the longest x5 12 us: body(): jnp.dot(columns, factor, preferred_element_type=jnp.float32)]
    ppermute x15 -> x0, starting transfers between devices: 19.6 us -> none  [from_partner(): return lax.ppermute(value, axis, pairs)]
    all_gather x1 -> x0, blocking collectives: 14.6 us -> none  [body(): outer_slots = lax.all_gather(head_slot, 'outer', axis=0, tiled=True)]
    all_gather x1 -> x0, waiting for transfers between devices: 10.5 us -> none  [body(): group_slots = lax.all_gather(coupling, 'inner', axis=0, tiled=True)]
    select_n x6 -> x0, other arithmetic: 6.09 us -> none  [the longest x5 5.17 us: body(): first_half = jnp.where(side_bit == 0, subtotal, sibling)]
  transfers between devices with their start and end apart: 16 -> 0, of which waited for: 15 -> 0; matrix products, arithmetic and copies ran while one was open for 6% -> 0% of each run, Pallas kernels for 0% -> 0%
where the time goes in v1:
time: 71.9 us; the launch traced here: 71.3 us
  Pallas kernels  68 us (95%)
  local copies, waits for them, and re-layouts  3.23 us (4%)
    pallas_call x1, Pallas kernels, body(): pl.pallas_call(functools.partial(sweep_kernel, bits_inner, levels, rank,...  64.4 us
    pallas_call x1, Pallas kernels, body(): pl.pallas_call(functools.partial(apply_kernel, wide), grid=(leaf // tile,...  3.61 us
    unnamed x8, local copies, waits for them, and re-layouts  3.23 us

profile of v1, /device:TPU:1, one launch (start us, length us, event | category | flops | bytes accessed | tf_op | source)
XLA Modules:
  0.0 71.3 jit_solution(9727142973358012110)
XLA Ops:
  0.0 0.0 copy-start
  0.0 0.0 copy-start.3
  0.0 64.4 %tree_sweep.1 = (f32[1024,768]{1,0:T(8,128)}, bf16[768,896]{1,0:T(8,128)(2,1)}) custom-call(f32[1024,768]{1,0:T(8,128)} %observed.1, s32[1,1024]{1,0:T(1,128)} %order.1, bf16[1024,1024]{1,0:T(8,128)(2,1)} %inverse.1, bf16[1024,640]{1,0:T(8,128)(2,1)} %project.1, bf16[1024,640]{1,0:T(8,128)(2,1)} %correct.3, bf16[256,256]{1,0:T(8,128)(2,1)} %coupling.1, ...), custom_call_target="tpu_custom_call" | custom-call | tf_op jit(solution)/shard_map/tree_sweep/pallas_call | solution.py:342
  64.4 0.0 copy-done
  64.4 0.0 copy-done.3
  64.4 0.0 copy-start.1
  64.4 1.9 %copy-done.1 = f32[1024,768]{1,0:T(8,128)S(1)} copy-done((f32[1024,768]{1,0:T(8,128)S(1)}, f32[1024,768]{1,0:T(8,128)}, u32[]{:S(2)}) %copy-start.1) | copy-done | bytes 3145752
  66.3 0.0 copy-start.2
  66.3 1.3 %copy-done.2 = bf16[768,896]{1,0:T(8,128)(2,1)S(1)} copy-done((bf16[768,896]{1,0:T(8,128)(2,1)S(1)}, bf16[768,896]{1,0:T(8,128)(2,1)}, u32[]{:S(2)}) %copy-start.2) | copy-done | bytes 1376280
  67.7 3.6 %apply_factors.1 = f32[1024,768]{1,0:T(8,128)} custom-call(f32[1024,768]{1,0:T(8,128)S(1)} %copy-done.1, bf16[1024,640]{1,0:T(8,128)(2,1)S(1)} %copy-done, bf16[1024,256]{1,0:T(8,128)(2,1)S(1)} %copy-done.3, bf16[768,896]{1,0:T(8,128)(2,1)S(1)} %copy-done.2), custom_call_target="tpu_custom_call" | custom-call | tf_op jit(solution)/shard_map/apply_factors/pallas_call | solution.py:356
Async XLA Ops:
  0.0 64.4 %copy-start = (bf16[1024,640]{1,0:T(8,128)(2,1)S(1)}, bf16[1024,640]{1,0:T(8,128)(2,1)}, u32[]{:S(2)}) copy-start(bf16[1024,640]{1,0:T(8,128)(2,1)} %correct.3) | copy-start | bytes 3932164
  0.0 64.4 %copy-start.3 = (bf16[1024,256]{1,0:T(8,128)(2,1)S(1)}, bf16[1024,256]{1,0:T(8,128)(2,1)}, u32[]{:S(2)}) copy-start(bf16[1024,256]{1,0:T(8,128)(2,1)} %trend.3) | copy-start | bytes 1572868
  64.4 1.9 %copy-start.1 = (f32[1024,768]{1,0:T(8,128)S(1)}, f32[1024,768]{1,0:T(8,128)}, u32[]{:S(2)}) copy-start(f32[1024,768]{1,0:T(8,128)} %get-tuple-element.7.estimate) | copy-start | bytes 9437188
  66.3 1.3 %copy-start.2 = (bf16[768,896]{1,0:T(8,128)(2,1)S(1)}, bf16[768,896]{1,0:T(8,128)(2,1)}, u32[]{:S(2)}) copy-start(bf16[768,896]{1,0:T(8,128)(2,1)} %get-tuple-element.8.factors) | copy-start | bytes 4128772

commit v2 on v1

v2 whole, which is shorter than its diff:
```python
import functools

import jax
import jax.numpy as jnp
from jax import lax
from jax.experimental import pallas as pl
from jax.experimental.pallas import tpu as pltpu
from jax.sharding import PartitionSpec as P

MESH = pl.DeviceIdType.MESH
BF = jnp.bfloat16
F32 = jnp.float32
NT = (((1,), (1,)), ((), ()))


def dot(a, b):
    return jnp.dot(a, b, preferred_element_type=F32)


def dot_nt(a, b):
    return lax.dot_general(a, b, NT, preferred_element_type=F32)


def plan(cols, levels, rank, trend):
    held, part = [], []
    now = cols
    for _ in range(levels):
        held.append(now)
        if now % 32 == 0:
            now //= 2
        part.append(now)
    rows = [(levels - s) * rank + trend for s in range(levels + 1)]
    width = [sum(rows[s + 1 :]) for s in range(levels)]
    return held, part, rows, width


def sweep_kernel(
    bits_inner,
    levels,
    rank,
    group,
    tile,
    observed,
    order,
    inverse,
    project,
    correct,
    coupling,
    trend,
    estimate_out,
    factor_out,
    obs_v,
    obs_bf,
    order_v,
    inv_v,
    basis_v,
    correct_v,
    hot_v,
    est_v,
    est_t,
    blocks,
    factors,
    gram_local,
    *rest,
):
    leaf, cols = observed.shape
    trend_rank = trend.shape[1]
    groups = cols // group
    held, part, rows, width = plan(group, levels, rank, trend_rank)
    rest = list(rest)

    def take(n):
        taken = rest[:n]
        del rest[:n]
        return taken

    sums = [take(levels + 1) for _ in range(groups)]
    x_send = [take(levels) for _ in range(groups)]
    x_recv = [take(levels) for _ in range(groups)]
    sib = [take(levels) for _ in range(groups)]
    gram = take(levels)
    gram_rest = take(levels - 1)
    gram_in = take(levels - 1)
    local_sem, send_sem, recv_sem = rest

    outer, inner = lax.axis_index("outer"), lax.axis_index("inner")
    bits, partners = [], []
    for s in range(levels):
        if s < bits_inner:
            span = 1 << s
            bit = lax.rem(inner // span, 2)
            partners.append((outer, inner + (1 - 2 * bit) * span))
        else:
            span = 1 << (s - bits_inner)
            bit = lax.rem(outer // span, 2)
            partners.append((outer + (1 - 2 * bit) * span, inner))
        bits.append(bit)
    side = bits[0]

    def local(src, dst, i):
        copy = pltpu.make_async_copy(src, dst, local_sem.at[i])
        copy.start()
        return copy

    wide = levels * rank
    c_block = local(coupling, blocks.at[0], 0)
    c_correct = local(correct, correct_v, 1)
    c_project = local(project, basis_v.at[:, pl.ds(0, wide)], 2)
    c_trend = local(trend, basis_v.at[:, pl.ds(wide, trend_rank)], 3)
    c_order = local(order, order_v, 4)
    c_inv = local(inverse, inv_v, 5)
    c_obs = local(observed, obs_v, 6)

    barrier = pltpu.get_barrier_semaphore()
    for partner in partners:
        pl.semaphore_signal(barrier, inc=1, device_id=partner, device_id_type=MESH)
    pl.semaphore_wait(barrier, levels)

    sent = []

    def remote(src, dst, kind, s, to):
        copy = pltpu.make_async_remote_copy(
            src_ref=src,
            dst_ref=dst,
            send_sem=send_sem.at[kind, s],
            recv_sem=recv_sem.at[kind, s],
            device_id=partners[to],
            device_id_type=MESH,
        )
        copy.start()
        sent.append(copy)
        return copy

    block_rows = coupling.shape[0] // 2
    gram_rows = rank // 2
    my_block = pl.ds(pl.multiple_of(side * block_rows, block_rows), block_rows)
    my_gram = pl.ds(pl.multiple_of(side * gram_rows, gram_rows), gram_rows)
    move = {}
    pending = jnp.int32(0)
    block_of = []

    def send_block(s):
        if s == 0:
            move["block", s] = remote(blocks.at[0], blocks.at[1], 0, s, s)
        else:
            place = blocks.at[s + 1, my_block]
            move["block", s] = remote(blocks.at[pending, my_block], place, 0, s, s)

    def send_gram(s):
        if s == 0:
            move["gram", s] = remote(gram[0].at[0], gram[0].at[1], 2, s, s)
            if levels > 1:
                move["rest", s] = remote(gram_local.at[1 - side], gram_in[0], 3, s, s)
            return
        mine = gram[s].at[0, my_gram]
        move["gram", s] = remote(mine, gram[s].at[1, my_gram], 2, s, s)
        if s + 1 < levels:
            move["rest", s] = remote(gram_rest[s], gram_in[s], 3, s, s)
        move["own", s] = remote(mine, mine, 4, s, 0)

    def advance(s):
        nonlocal pending
        move["block", s].wait_recv()
        block_of.append(jnp.where(bits[s] == 1, pending, s + 1))
        pending = jnp.where(bits[s] == 1, s + 1, pending)
        if s + 1 < levels:
            send_block(s + 1)
            move["rest", s].wait_recv()
            here = gram_local[side] if s == 0 else gram_rest[s][...]
            total = (here.astype(F32) + gram_in[s][...].astype(F32)).astype(BF)
            skip = rows[s + 2]
            gram[s + 1][0, my_gram, :] = total[:, :skip]
            if s + 2 < levels:
                gram_rest[s + 1][...] = total[:, skip:]
            send_gram(s + 1)
        move["gram", s].wait_recv()
        if s > 0:
            block = blocks.at[s + 1, my_block]
            move["block2", s] = remote(block, block, 1, s, 0)
            other = gram[s].at[1, my_gram]
            move["other", s] = remote(other, other, 5, s, 0)

    def ready(s):
        if s > 0:
            move["block2", s].wait_recv()
            move["own", s].wait_recv()
            move["other", s].wait_recv()

    c_block.wait()
    send_block(0)

    c_correct.wait()
    c_project.wait()
    c_trend.wait()
    at = 0
    for s in range(levels):
        columns_t = correct_v[:, s * rank : (s + 1) * rank].T
        value = dot(columns_t, basis_v[:, (s + 1) * rank :]).astype(BF)
        if s == 0:
            gram[0][0] = value
        else:
            gram_local[0, :, at : at + rows[s + 1]] = value[:gram_rows]
            gram_local[1, :, at : at + rows[s + 1]] = value[gram_rows:]
            at += rows[s + 1]
    send_gram(0)

    c_order.wait()
    steps = leaf // tile

    def make_hot(t, carry):
        r0 = pl.multiple_of(t * tile, tile)
        ids = lax.broadcasted_iota(jnp.int32, (tile, leaf), 0) + r0
        hot_v[pl.ds(r0, tile), :] = jnp.where(ids == order_v[...], 1.0, 0.0).astype(BF)
        return carry

    lax.fori_loop(0, steps, make_hot, 0)
    advance(0)
    c_inv.wait()

    def reorder(t, carry):
        r0 = pl.multiple_of(t * tile, tile)
        value = dot_nt(inv_v[pl.ds(r0, tile), :], hot_v[...]).astype(BF)
        inv_v[pl.ds(r0, tile), :] = value
        return carry

    lax.fori_loop(0, steps, reorder, 0)
    c_obs.wait()

    x_move, sib_move, down_move = {}, {}, {}
    offsets = [[jnp.int32(g * group)] for g in range(groups)]
    finals = []

    def send_x(g, s):
        x_move[g, s] = remote(x_send[g][s], x_recv[g][s], 6 + g, s, s)

    def start_group(g):
        lanes = slice(g * group, (g + 1) * group)

        def make_estimate(t, carry):
            r0 = pl.multiple_of(t * tile, tile)
            value = dot(inv_v[pl.ds(r0, tile), :], obs_bf[:, lanes])
            est_v[pl.ds(r0, tile), lanes] = value
            est_t[lanes, pl.ds(r0, tile)] = value.astype(BF).T
            return carry

        obs_bf[:, lanes] = obs_v[:, lanes].astype(BF)
        lax.fori_loop(0, steps, make_estimate, 0)
        half = part[0]
        away = pl.ds(pl.multiple_of(g * group + (1 - side) * half, half), half)
        x_send[g][0][...] = dot(est_t[away, :], basis_v[...]).astype(BF)
        send_x(g, 0)
        keep = pl.ds(pl.multiple_of(g * group + side * half, half), half)
        sums[g][0][...] = dot(est_t[keep, :], basis_v[...])

    def up(g, s):
        count = part[s]
        halves = held[s] != part[s]
        first_side = bits[s] == 0
        offset = offsets[g][s] + (bits[s] * count if halves else 0)
        offset = pl.multiple_of(offset, count)
        offsets[g].append(offset)
        if s == 0 or not halves:
            own = sums[g][s][...]
        else:
            own = sums[g][s][pl.ds(pl.multiple_of(bits[s] * count, count), count), :]
        x_move[g, s].wait_recv()
        if g == 0:
            ready(s)
        other = x_recv[g][s][...].astype(F32)
        own_head, other_head = own[:, :rank], other[:, :rank]
        one = jnp.where(first_side, own_head, other_head).astype(BF)
        two = jnp.where(first_side, other_head, own_head).astype(BF)
        block = blocks[block_of[s]]
        factor = dot_nt(one, block[:, :rank]) + dot_nt(two, block[:, rank:])
        mine = jnp.where(first_side, factor[:, :rank], factor[:, rank:]).astype(BF)
        theirs = jnp.where(first_side, factor[:, rank:], factor[:, :rank]).astype(BF)
        new = (
            own[:, rank:]
            + other[:, rank:]
            - dot(mine, gram[s][0])
            - dot(theirs, gram[s][1])
        )
        sums[g][s + 1][...] = new
        if s + 1 < levels:
            after = part[s + 1]
            if held[s + 1] != after:
                away = pl.multiple_of((1 - bits[s + 1]) * after, after)
                x_send[g][s + 1][...] = sums[g][s + 1][pl.ds(away, after), :].astype(BF)
            else:
                x_send[g][s + 1][...] = new.astype(BF)
            send_x(g, s + 1)
        factors[pl.ds(offset, count), s * rank : (s + 1) * rank] = mine
        if halves:
            sib[g][s][...] = theirs
            place = factors.at[pl.ds(offset, count), pl.ds(s * rank, rank)]
            sib_move[g, s] = remote(sib[g][s], place, 6 + groups + g, s, s)
        if s + 1 == levels:
            trend_factor = dot_nt(new.astype(BF), blocks[pending]).astype(BF)
            factors[pl.ds(offset, count), wide:] = trend_factor
            send_down(g, 0)

    split = [s for s in reversed(range(levels)) if held[s] != part[s]]

    def send_down(g, i):
        s = split[i]
        lanes = pl.ds((s + 1) * rank, rows[s + 1])
        place = factors.at[pl.ds(offsets[g][s + 1], part[s]), lanes]
        down_move[g, i] = remote(place, place, 6 + 2 * groups + g, s, s)

    def down(g, i):
        down_move[g, i].wait_recv()
        sib_move[g, split[i]].wait_recv()
        if i + 1 < len(split):
            send_down(g, i + 1)
        else:
            mine = pl.ds(g * group, group)
            finals.append(local(factors.at[mine], factor_out.at[mine], 8 + g))

    last = 1 + levels + len(split)
    for wave in range(last + groups - 1):
        for g in reversed(range(groups)):
            step = wave - g
            if step < 0 or step >= last:
                continue
            if step == 0:
                start_group(g)
                if g == groups - 1:
                    finals.append(local(est_v, estimate_out, 7))
            elif step <= levels:
                if g == 0 and step > 1:
                    advance(step - 1)
                up(g, step - 1)
            else:
                down(g, step - 1 - levels)

    for copy in sent:
        copy.wait_send()
    for copy in finals:
        copy.wait()


def apply_kernel(wide, estimate, correct, trend, factors, out):
    out[...] = (
        estimate[...]
        - dot_nt(correct[...], factors[:, :wide])
        - dot_nt(trend[...], factors[:, wide:])
    )


def body(
    bits_inner,
    levels,
    observed,
    leaf_order,
    leaf_inverse,
    project_basis,
    correct_basis,
    coupling,
    trend_basis,
    trend_correct,
):
    leaf, cols = observed.shape
    wide = correct_basis.shape[1]
    rank = wide // levels
    trend_rank = trend_basis.shape[1]
    group = 256 if cols % 256 == 0 else cols
    groups = cols // group
    held, part, rows, width = plan(group, levels, rank, trend_rank)
    tile = 256 if leaf % 256 == 0 else leaf
    vm = pltpu.VMEM
    every = range(levels)
    scratch = [
        vm((leaf, cols), F32),
        vm((leaf, cols), BF),
        vm(leaf_order.shape, jnp.int32),
        vm((leaf, leaf), BF),
        vm((leaf, wide + trend_rank), BF),
        vm((leaf, wide), BF),
        vm((leaf, leaf), BF),
        vm((leaf, cols), F32),
        vm((cols, leaf), BF),
        vm((levels + 1,) + coupling.shape, BF),
        vm((cols, wide + trend_rank), BF),
        vm((2, rank // 2, max(width[0] - rows[1], rank)), BF),
    ]
    for _ in range(groups):
        scratch += [vm((part[0], rows[0]), F32)]
        scratch += [vm((part[s], rows[s + 1]), F32) for s in every]
    scratch += [vm((part[s], rows[s]), BF) for s in every] * (2 * groups)
    scratch += [vm((part[s], rank), BF) for s in every] * groups
    scratch += [vm((2, rank, rows[s + 1]), BF) for s in every]
    scratch += [vm((rank // 2, width[s + 1]), BF) for s in range(levels - 1)] * 2
    scratch += [
        pltpu.SemaphoreType.DMA((8 + groups,)),
        pltpu.SemaphoreType.DMA((6 + 3 * groups, levels)),
        pltpu.SemaphoreType.DMA((6 + 3 * groups, levels)),
    ]
    anywhere = pl.BlockSpec(memory_space=pl.ANY)
    estimate, factors = pl.pallas_call(
        functools.partial(sweep_kernel, bits_inner, levels, rank, group, tile),
        out_shape=(
            jax.ShapeDtypeStruct((leaf, cols), F32),
            jax.ShapeDtypeStruct((cols, wide + trend_rank), BF),
        ),
        in_specs=[anywhere] * 7,
        out_specs=(anywhere, anywhere),
        scratch_shapes=scratch,
        compiler_params=pltpu.CompilerParams(
            collective_id=0, has_side_effects=True, vmem_limit_bytes=56 * 1024 * 1024
        ),
        name="tree_sweep",
    )(observed, leaf_order, leaf_inverse, project_basis, correct_basis, coupling, trend_basis)
    return pl.pallas_call(
        functools.partial(apply_kernel, wide),
        grid=(leaf // tile,),
        out_shape=jax.ShapeDtypeStruct((leaf, cols), F32),
        in_specs=[
            pl.BlockSpec((tile, cols), lambda i: (i, 0)),
            pl.BlockSpec((tile, wide), lambda i: (i, 0)),
            pl.BlockSpec((tile, trend_rank), lambda i: (i, 0)),
            pl.BlockSpec((cols, wide + trend_rank), lambda i: (0, 0)),
        ],
        out_specs=pl.BlockSpec((tile, cols), lambda i: (i, 0)),
        compiler_params=pltpu.CompilerParams(vmem_limit_bytes=62 * 1024 * 1024),
        name="apply_factors",
    )(estimate, correct_basis, trend_correct, factors)


def solution(mesh):
    bits_inner = mesh.shape["inner"].bit_length() - 1
    bits_outer = mesh.shape["outer"].bit_length() - 1
    rows = P(("outer", "inner"), None)
    return jax.shard_map(
        functools.partial(body, bits_inner, bits_inner + bits_outer),
        mesh=mesh,
        in_specs=(rows,) * 8,
        out_specs=rows,
        check_vma=False,
    )
```

time: 71.9 us -> 58.1 us (0.81)
  Pallas kernels: 68 us -> 57.9 us
  local copies, waits for them, and re-layouts: 3.23 us -> 0 us
    pallas_call x1, Pallas kernels: 64.4 us -> 51.6 us  [body(): pl.pallas_call(functools.partial(sweep_kernel, bits_inner, levels, rank,...]
    unnamed x8 -> x0, local copies, waits for them, and re-layouts: 3.23 us -> none
    pallas_call x1, Pallas kernels: 3.61 us -> 6.22 us  [body(): pl.pallas_call(functools.partial(apply_kernel, wide), grid=(leaf // tile,...]
where the time goes in v2:
time: 58.1 us; the launch traced here: 57.9 us
  Pallas kernels  57.9 us (100%)
    pallas_call x1, Pallas kernels, body(): pl.pallas_call(functools.partial(sweep_kernel, bits_inner, levels, rank,...  51.6 us
    pallas_call x1, Pallas kernels, body(): pl.pallas_call(functools.partial(apply_kernel, wide), grid=(leaf // tile,...  6.22 us

profile of v2, /device:TPU:1, one launch (start us, length us, event | category | flops | bytes accessed | tf_op | source)
XLA Modules:
  0.0 57.9 jit_solution(4634000441048855536)
XLA Ops:
  0.0 51.6 %tree_sweep.1 = (f32[1024,768]{1,0:T(8,128)}, bf16[768,896]{1,0:T(8,128)(2,1)}) custom-call(f32[1024,768]{1,0:T(8,128)} %observed.1, s32[1,1024]{1,0:T(1,128)} %order.1, bf16[1024,1024]{1,0:T(8,128)(2,1)} %inverse.1, bf16[1024,640]{1,0:T(8,128)(2,1)} %project.1, bf16[1024,640]{1,0:T(8,128)(2,1)} %correct.3, bf16[256,256]{1,0:T(8,128)(2,1)} %coupling.1, ...), custom_call_target="tpu_custom_call" | custom-call | tf_op jit(solution)/shard_map/tree_sweep/pallas_call | solution.py:399
  51.7 6.2 %apply_factors.1 = f32[1024,768]{1,0:T(8,128)} custom-call(f32[1024,768]{1,0:T(8,128)} %get-tuple-element.7.estimate, bf16[1024,640]{1,0:T(8,128)(2,1)} %correct.3, bf16[1024,256]{1,0:T(8,128)(2,1)} %trend.3, bf16[768,896]{1,0:T(8,128)(2,1)} %get-tuple-element.8.factors), custom_call_target="tpu_custom_call" | custom-call | tf_op jit(solution)/shard_map/apply_factors/pallas_call | solution.py:413

commit v3 on v2

--- a/solution.py
+++ b/solution.py
@@ -47,14 +47,15 @@
     correct,
     coupling,
     trend,
-    estimate_out,
-    factor_out,
+    trend_correct,
+    out,
     obs_v,
     obs_bf,
     order_v,
     inv_v,
     basis_v,
     correct_v,
+    trend_v,
     hot_v,
     est_v,
     est_t,
@@ -108,8 +109,6 @@
     c_project = local(project, basis_v.at[:, pl.ds(0, wide)], 2)
     c_trend = local(trend, basis_v.at[:, pl.ds(wide, trend_rank)], 3)
     c_order = local(order, order_v, 4)
-    c_inv = local(inverse, inv_v, 5)
-    c_obs = local(observed, obs_v, 6)
 
     barrier = pltpu.get_barrier_semaphore()
     for partner in partners:
@@ -148,35 +147,42 @@
 
     def send_gram(s):
         if s == 0:
-            move["gram", s] = remote(gram[0].at[0], gram[0].at[1], 2, s, s)
             if levels > 1:
                 move["rest", s] = remote(gram_local.at[1 - side], gram_in[0], 3, s, s)
+            move["gram", s] = remote(gram[0].at[0], gram[0].at[1], 2, s, s)
             return
+        if s + 1 < levels:
+            move["rest", s] = remote(gram_rest[s], gram_in[s], 3, s, s)
         mine = gram[s].at[0, my_gram]
         move["gram", s] = remote(mine, gram[s].at[1, my_gram], 2, s, s)
-        if s + 1 < levels:
-            move["rest", s] = remote(gram_rest[s], gram_in[s], 3, s, s)
         move["own", s] = remote(mine, mine, 4, s, 0)
 
-    def advance(s):
+    def advance_block(s):
         nonlocal pending
         move["block", s].wait_recv()
         block_of.append(jnp.where(bits[s] == 1, pending, s + 1))
         pending = jnp.where(bits[s] == 1, s + 1, pending)
         if s + 1 < levels:
             send_block(s + 1)
-            move["rest", s].wait_recv()
-            here = gram_local[side] if s == 0 else gram_rest[s][...]
-            total = (here.astype(F32) + gram_in[s][...].astype(F32)).astype(BF)
-            skip = rows[s + 2]
-            gram[s + 1][0, my_gram, :] = total[:, :skip]
-            if s + 2 < levels:
-                gram_rest[s + 1][...] = total[:, skip:]
-            send_gram(s + 1)
-        move["gram", s].wait_recv()
         if s > 0:
             block = blocks.at[s + 1, my_block]
             move["block2", s] = remote(block, block, 1, s, 0)
+
+    def advance_gram(s):
+        if s + 1 >= levels:
+            return
+        move["rest", s].wait_recv()
+        here = gram_local[side] if s == 0 else gram_rest[s][...]
+        total = (here.astype(F32) + gram_in[s][...].astype(F32)).astype(BF)
+        skip = rows[s + 2]
+        if s + 2 < levels:
+            gram_rest[s + 1][...] = total[:, skip:]
+        gram[s + 1][0, my_gram, :] = total[:, :skip]
+        send_gram(s + 1)
+
+    def share_gram(s):
+        move["gram", s].wait_recv()
+        if s > 0:
             other = gram[s].at[1, my_gram]
             move["other", s] = remote(other, other, 5, s, 0)
 
@@ -192,17 +198,24 @@
     c_correct.wait()
     c_project.wait()
     c_trend.wait()
+    c_inv = local(inverse, inv_v, 5)
+    c_obs = local(observed, obs_v, 6)
+    c_last = local(trend_correct, trend_v, 7)
     at = 0
-    for s in range(levels):
-        columns_t = correct_v[:, s * rank : (s + 1) * rank].T
-        value = dot(columns_t, basis_v[:, (s + 1) * rank :]).astype(BF)
-        if s == 0:
-            gram[0][0] = value
-        else:
-            gram_local[0, :, at : at + rows[s + 1]] = value[:gram_rows]
-            gram_local[1, :, at : at + rows[s + 1]] = value[gram_rows:]
-            at += rows[s + 1]
+    for s in range(0, levels, 2):
+        both = min(2, levels - s)
+        columns_t = correct_v[:, s * rank : (s + both) * rank].T
+        pair = dot(columns_t, basis_v[:, (s + 1) * rank :]).astype(BF)
+        for u in range(both):
+            value = pair[u * rank : (u + 1) * rank, u * rank :]
+            if s + u == 0:
+                gram[0][0] = value
+            else:
+                gram_local[0, :, at : at + rows[s + u + 1]] = value[:gram_rows]
+                gram_local[1, :, at : at + rows[s + u + 1]] = value[gram_rows:]
+                at += rows[s + u + 1]
     send_gram(0)
+    advance_block(0)
 
     c_order.wait()
     steps = leaf // tile
@@ -214,7 +227,7 @@
         return carry
 
     lax.fori_loop(0, steps, make_hot, 0)
-    advance(0)
+    advance_gram(0)
     c_inv.wait()
 
     def reorder(t, carry):
@@ -224,7 +237,10 @@
         return carry
 
     lax.fori_loop(0, steps, reorder, 0)
+    if levels > 1:
+        advance_block(1)
     c_obs.wait()
+    c_last.wait()
 
     x_move, sib_move, down_move = {}, {}, {}
     offsets = [[jnp.int32(g * group)] for g in range(groups)]
@@ -245,12 +261,13 @@
 
         obs_bf[:, lanes] = obs_v[:, lanes].astype(BF)
         lax.fori_loop(0, steps, make_estimate, 0)
-        half = part[0]
-        away = pl.ds(pl.multiple_of(g * group + (1 - side) * half, half), half)
-        x_send[g][0][...] = dot(est_t[away, :], basis_v[...]).astype(BF)
+        sums[g][0][...] = dot(est_t[lanes, :], basis_v[...])
+        if held[0] != part[0]:
+            away = pl.ds(pl.multiple_of((1 - side) * part[0], part[0]), part[0])
+            x_send[g][0][...] = sums[g][0][away, :].astype(BF)
+        else:
+            x_send[g][0][...] = sums[g][0][...].astype(BF)
         send_x(g, 0)
-        keep = pl.ds(pl.multiple_of(g * group + side * half, half), half)
-        sums[g][0][...] = dot(est_t[keep, :], basis_v[...])
 
     def up(g, s):
         count = part[s]
@@ -259,7 +276,7 @@
         offset = offsets[g][s] + (bits[s] * count if halves else 0)
         offset = pl.multiple_of(offset, count)
         offsets[g].append(offset)
-        if s == 0 or not halves:
+        if not halves:
             own = sums[g][s][...]
         else:
             own = sums[g][s][pl.ds(pl.multiple_of(bits[s] * count, count), count), :]
@@ -313,8 +330,24 @@
         if i + 1 < len(split):
             send_down(g, i + 1)
         else:
-            mine = pl.ds(g * group, group)
-            finals.append(local(factors.at[mine], factor_out.at[mine], 8 + g))
+            finish(g)
+
+    def finish(g):
+        lanes = slice(g * group, (g + 1) * group)
+
+        def apply(t, carry):
+            r0 = pl.multiple_of(t * tile, tile)
+            place = pl.ds(r0, tile)
+            est_v[place, lanes] = (
+                est_v[place, lanes]
+                - dot_nt(correct_v[place, :], factors[lanes, :wide])
+                - dot_nt(trend_v[place, :], factors[lanes, wide:])
+            )
+            return carry
+
+        lax.fori_loop(0, steps, apply, 0)
+        mine = pl.ds(g * group, group)
+        finals.append(local(est_v.at[:, mine], out.at[:, mine], 8 + g))
 
     last = 1 + levels + len(split)
     for wave in range(last + groups - 1):
@@ -324,12 +357,17 @@
                 continue
             if step == 0:
                 start_group(g)
-                if g == groups - 1:
-                    finals.append(local(est_v, estimate_out, 7))
             elif step <= levels:
-                if g == 0 and step > 1:
-                    advance(step - 1)
+                if g == 0:
+                    if step + 1 < levels:
+                        advance_block(step + 1)
+                    if step < levels:
+                        advance_gram(step)
+                    if step == 1:
+                        share_gram(0)
                 up(g, step - 1)
+                if g == 0 and step < levels:
+                    share_gram(step)
             else:
                 down(g, step - 1 - levels)
 
@@ -337,14 +375,6 @@
         copy.wait_send()
     for copy in finals:
         copy.wait()
-
-
-def apply_kernel(wide, estimate, correct, trend, factors, out):
-    out[...] = (
-        estimate[...]
-        - dot_nt(correct[...], factors[:, :wide])
-        - dot_nt(trend[...], factors[:, wide:])
-    )
 
 
 def body(
@@ -366,7 +396,7 @@
     group = 256 if cols % 256 == 0 else cols
     groups = cols // group
     held, part, rows, width = plan(group, levels, rank, trend_rank)
-    tile = 256 if leaf % 256 == 0 else leaf
+    tile = 512 if leaf % 512 == 0 else leaf
     vm = pltpu.VMEM
     every = range(levels)
     scratch = [
@@ -376,6 +406,7 @@
         vm((leaf, leaf), BF),
         vm((leaf, wide + trend_rank), BF),
         vm((leaf, wide), BF),
+        vm((leaf, trend_rank), BF),
         vm((leaf, leaf), BF),
         vm((leaf, cols), F32),
         vm((cols, leaf), BF),
@@ -384,7 +415,7 @@
         vm((2, rank // 2, max(width[0] - rows[1], rank)), BF),
     ]
     for _ in range(groups):
-        scratch += [vm((part[0], rows[0]), F32)]
+        scratch += [vm((held[0], rows[0]), F32)]
         scratch += [vm((part[s], rows[s + 1]), F32) for s in every]
     scratch += [vm((part[s], rows[s]), BF) for s in every] * (2 * groups)
     scratch += [vm((part[s], rank), BF) for s in every] * groups
@@ -395,35 +426,26 @@
         pltpu.SemaphoreType.DMA((6 + 3 * groups, levels)),
         pltpu.SemaphoreType.DMA((6 + 3 * groups, levels)),
     ]
-    anywhere = pl.BlockSpec(memory_space=pl.ANY)
-    estimate, factors = pl.pallas_call(
+    return pl.pallas_call(
         functools.partial(sweep_kernel, bits_inner, levels, rank, group, tile),
-        out_shape=(
-            jax.ShapeDtypeStruct((leaf, cols), F32),
-            jax.ShapeDtypeStruct((cols, wide + trend_rank), BF),
-        ),
-        in_specs=[anywhere] * 7,
-        out_specs=(anywhere, anywhere),
+        out_shape=jax.ShapeDtypeStruct((leaf, cols), F32),
+        in_specs=[pl.BlockSpec(memory_space=pltpu.HBM)] * 8,
+        out_specs=pl.BlockSpec(memory_space=pl.ANY),
         scratch_shapes=scratch,
         compiler_params=pltpu.CompilerParams(
             collective_id=0, has_side_effects=True, vmem_limit_bytes=56 * 1024 * 1024
         ),
         name="tree_sweep",
-    )(observed, leaf_order, leaf_inverse, project_basis, correct_basis, coupling, trend_basis)
-    return pl.pallas_call(
-        functools.partial(apply_kernel, wide),
-        grid=(leaf // tile,),
-        out_shape=jax.ShapeDtypeStruct((leaf, cols), F32),
-        in_specs=[
-            pl.BlockSpec((tile, cols), lambda i: (i, 0)),
-            pl.BlockSpec((tile, wide), lambda i: (i, 0)),
-            pl.BlockSpec((tile, trend_rank), lambda i: (i, 0)),
-            pl.BlockSpec((cols, wide + trend_rank), lambda i: (0, 0)),
-        ],
-        out_specs=pl.BlockSpec((tile, cols), lambda i: (i, 0)),
-        compiler_params=pltpu.CompilerParams(vmem_limit_bytes=62 * 1024 * 1024),
-        name="apply_factors",
-    )(estimate, correct_basis, trend_correct, factors)
+    )(
+        observed,
+        leaf_order,
+        leaf_inverse,
+        project_basis,
+        correct_basis,
+        coupling,
+        trend_basis,
+        trend_correct,
+    )
 
 
 def solution(mesh):

time: 58.1 us -> 51.8 us (0.89)
  Pallas kernels: 57.9 us -> 47.9 us
  local copies, waits for them, and re-layouts: 0 us -> 3.76 us
    pallas_call x1 -> x0, Pallas kernels: 6.22 us -> none  [body(): pl.pallas_call(functools.partial(apply_kernel, wide), grid=(leaf // tile,...]
    unnamed x0 -> x1, local copies, waits for them, and re-layouts: none -> 3.76 us
    pallas_call x1, Pallas kernels: 51.6 us -> 47.9 us  [body(): pl.pallas_call(functools.partial(sweep_kernel, bits_inner, levels, rank,...]
where the time goes in v3:
time: 51.8 us; the launch traced here: 51.7 us
  Pallas kernels  47.9 us (92%)
  local copies, waits for them, and re-layouts  3.76 us (7%)
    pallas_call x1, Pallas kernels, body(): pl.pallas_call(functools.partial(sweep_kernel, bits_inner, levels, rank,...  47.9 us
    unnamed x1, local copies, waits for them, and re-layouts  3.76 us

profile of v3, /device:TPU:1, one launch (start us, length us, event | category | flops | bytes accessed | tf_op | source)
XLA Modules:
  0.0 51.7 jit_solution(11292792906321956105)
XLA Ops:
  0.0 47.9 %tree_sweep.1 = f32[1024,768]{1,0:T(8,128)} custom-call(f32[1024,768]{1,0:T(8,128)} %observed.1, s32[1,1024]{1,0:T(1,128)} %order.1, bf16[1024,1024]{1,0:T(8,128)(2,1)} %inverse.1, bf16[1024,640]{1,0:T(8,128)(2,1)} %project.1, bf16[1024,640]{1,0:T(8,128)(2,1)} %correct.1, bf16[256,256]{1,0:T(8,128)(2,1)} %coupling.1, bf16[1024,256]{1,0:T(8,128)(2,1)} %trend.1, ...), custom_call_target="tpu_custom_call" | custom-call | tf_op jit(solution)/shard_map/tree_sweep/pallas_call | solution.py:429
  47.9 3.8 %copy.10 = f32[1024,768]{1,0:T(8,128)} copy(f32[1024,768]{1,0:T(8,128)} %tree_sweep.1) | data formatting | bytes 6291456

commit v4 on v3

--- a/solution.py
+++ b/solution.py
@@ -57,6 +57,8 @@
     correct_v,
     trend_v,
     hot_v,
+    column_v,
+    ordered_v,
     est_v,
     est_t,
     blocks,
@@ -97,6 +99,23 @@
             partners.append((outer + (1 - 2 * bit) * span, inner))
         bits.append(bit)
     side = bits[0]
+    split = [s for s in range(levels) if held[s] != part[s]]
+    late = len(split)
+
+    def across(mask):
+        to_outer, to_inner = outer, inner
+        for s in range(levels):
+            if mask >> s & 1:
+                if s < bits_inner:
+                    to_inner = to_inner + (1 - 2 * bits[s]) * (1 << s)
+                else:
+                    to_outer = to_outer + (1 - 2 * bits[s]) * (1 << (s - bits_inner))
+        return to_outer, to_inner
+
+    wide_masks = [m for m in range(2, 1 << late, 2)]
+    partners = {1 << s: partners[s] for s in range(levels)}
+    for mask in wide_masks:
+        partners.setdefault(mask, across(mask))
 
     def local(src, dst, i):
         copy = pltpu.make_async_copy(src, dst, local_sem.at[i])
@@ -111,19 +130,20 @@
     c_order = local(order, order_v, 4)
 
     barrier = pltpu.get_barrier_semaphore()
-    for partner in partners:
+    for partner in partners.values():
         pl.semaphore_signal(barrier, inc=1, device_id=partner, device_id_type=MESH)
-    pl.semaphore_wait(barrier, levels)
+    pl.semaphore_wait(barrier, len(partners))
 
     sent = []
 
-    def remote(src, dst, kind, s, to):
+    def remote(src, dst, mask):
+        slot = len(sent)
         copy = pltpu.make_async_remote_copy(
             src_ref=src,
             dst_ref=dst,
-            send_sem=send_sem.at[kind, s],
-            recv_sem=recv_sem.at[kind, s],
-            device_id=partners[to],
+            send_sem=send_sem.at[slot],
+            recv_sem=recv_sem.at[slot],
+            device_id=partners[mask],
             device_id_type=MESH,
         )
         copy.start()
@@ -140,22 +160,22 @@
 
     def send_block(s):
         if s == 0:
-            move["block", s] = remote(blocks.at[0], blocks.at[1], 0, s, s)
+            move["block", s] = remote(blocks.at[0], blocks.at[1], 1)
         else:
             place = blocks.at[s + 1, my_block]
-            move["block", s] = remote(blocks.at[pending, my_block], place, 0, s, s)
+            move["block", s] = remote(blocks.at[pending, my_block], place, 1 << s)
 
     def send_gram(s):
         if s == 0:
             if levels > 1:
-                move["rest", s] = remote(gram_local.at[1 - side], gram_in[0], 3, s, s)
-            move["gram", s] = remote(gram[0].at[0], gram[0].at[1], 2, s, s)
+                move["rest", s] = remote(gram_local.at[1 - side], gram_in[0], 1)
+            move["gram", s] = remote(gram[0].at[0], gram[0].at[1], 1)
             return
         if s + 1 < levels:
-            move["rest", s] = remote(gram_rest[s], gram_in[s], 3, s, s)
+            move["rest", s] = remote(gram_rest[s], gram_in[s], 1 << s)
         mine = gram[s].at[0, my_gram]
-        move["gram", s] = remote(mine, gram[s].at[1, my_gram], 2, s, s)
-        move["own", s] = remote(mine, mine, 4, s, 0)
+        move["gram", s] = remote(mine, gram[s].at[1, my_gram], 1 << s)
+        move["own", s] = remote(mine, mine, 1)
 
     def advance_block(s):
         nonlocal pending
@@ -166,7 +186,7 @@
             send_block(s + 1)
         if s > 0:
             block = blocks.at[s + 1, my_block]
-            move["block2", s] = remote(block, block, 1, s, 0)
+            move["block2", s] = remote(block, block, 1)
 
     def advance_gram(s):
         if s + 1 >= levels:
@@ -184,7 +204,7 @@
         move["gram", s].wait_recv()
         if s > 0:
             other = gram[s].at[1, my_gram]
-            move["other", s] = remote(other, other, 5, s, 0)
+            move["other", s] = remote(other, other, 1)
 
     def ready(s):
         if s > 0:
@@ -219,47 +239,52 @@
 
     c_order.wait()
     steps = leaf // tile
+    column_v[...] = jnp.broadcast_to(order_v[...].astype(F32), (128, leaf)).T
+    blocks_wide = leaf // 128
 
     def make_hot(t, carry):
-        r0 = pl.multiple_of(t * tile, tile)
-        ids = lax.broadcasted_iota(jnp.int32, (tile, leaf), 0) + r0
-        hot_v[pl.ds(r0, tile), :] = jnp.where(ids == order_v[...], 1.0, 0.0).astype(BF)
+        place = pl.ds(pl.multiple_of(t * 128, 128), 128)
+        column = column_v[place, :]
+        lane = lax.broadcasted_iota(jnp.int32, (128, 128), 1).astype(F32)
+        for k in range(blocks_wide):
+            hit = column == lane + float(128 * k)
+            hot_v[place, k * 128 : (k + 1) * 128] = jnp.where(hit, 1.0, 0.0).astype(BF)
         return carry
 
-    lax.fori_loop(0, steps, make_hot, 0)
+    lax.fori_loop(0, blocks_wide, make_hot, 0)
     advance_gram(0)
     c_inv.wait()
 
-    def reorder(t, carry):
-        r0 = pl.multiple_of(t * tile, tile)
-        value = dot_nt(inv_v[pl.ds(r0, tile), :], hot_v[...]).astype(BF)
-        inv_v[pl.ds(r0, tile), :] = value
-        return carry
-
-    lax.fori_loop(0, steps, reorder, 0)
     if levels > 1:
         advance_block(1)
     c_obs.wait()
     c_last.wait()
 
-    x_move, sib_move, down_move = {}, {}, {}
+    x_move, early, late_move, core_move = {}, {}, {}, {}
     offsets = [[jnp.int32(g * group)] for g in range(groups)]
     finals = []
 
     def send_x(g, s):
-        x_move[g, s] = remote(x_send[g][s], x_recv[g][s], 6 + g, s, s)
+        x_move[g, s] = remote(x_send[g][s], x_recv[g][s], 1 << s)
 
     def start_group(g):
         lanes = slice(g * group, (g + 1) * group)
 
+        def make_ordered(t, carry):
+            r0 = pl.multiple_of(t * tile, tile)
+            value = dot(hot_v[pl.ds(r0, tile), :], obs_bf[:, lanes])
+            ordered_v[pl.ds(r0, tile), :] = value.astype(BF)
+            return carry
+
         def make_estimate(t, carry):
             r0 = pl.multiple_of(t * tile, tile)
-            value = dot(inv_v[pl.ds(r0, tile), :], obs_bf[:, lanes])
+            value = dot(inv_v[pl.ds(r0, tile), :], ordered_v[...])
             est_v[pl.ds(r0, tile), lanes] = value
             est_t[lanes, pl.ds(r0, tile)] = value.astype(BF).T
             return carry
 
         obs_bf[:, lanes] = obs_v[:, lanes].astype(BF)
+        lax.fori_loop(0, steps, make_ordered, 0)
         lax.fori_loop(0, steps, make_estimate, 0)
         sums[g][0][...] = dot(est_t[lanes, :], basis_v[...])
         if held[0] != part[0]:
@@ -309,28 +334,43 @@
         factors[pl.ds(offset, count), s * rank : (s + 1) * rank] = mine
         if halves:
             sib[g][s][...] = theirs
-            place = factors.at[pl.ds(offset, count), pl.ds(s * rank, rank)]
-            sib_move[g, s] = remote(sib[g][s], place, 6 + groups + g, s, s)
         if s + 1 == levels:
             trend_factor = dot_nt(new.astype(BF), blocks[pending]).astype(BF)
             factors[pl.ds(offset, count), wide:] = trend_factor
-            send_down(g, 0)
-
-    split = [s for s in reversed(range(levels)) if held[s] != part[s]]
-
-    def send_down(g, i):
-        s = split[i]
-        lanes = pl.ds((s + 1) * rank, rows[s + 1])
-        place = factors.at[pl.ds(offsets[g][s + 1], part[s]), lanes]
-        down_move[g, i] = remote(place, place, 6 + 2 * groups + g, s, s)
-
-    def down(g, i):
-        down_move[g, i].wait_recv()
-        sib_move[g, split[i]].wait_recv()
-        if i + 1 < len(split):
-            send_down(g, i + 1)
-        else:
-            finish(g)
+            place = factors.at[pl.ds(offset, count), pl.ds(late * rank, rows[late])]
+            for mask in wide_masks:
+                late_move[g, mask] = remote(place, place, mask)
+        if halves:
+            place = factors.at[pl.ds(offset, count), pl.ds(s * rank, rank)]
+            masks = [1] if s == 0 else [m for m in wide_masks if m < 2 << s]
+            for mask in masks:
+                source = sib[g][s] if mask >> s & 1 else place
+                early[g, s, mask] = remote(source, place, mask)
+
+    def core_rows(g):
+        return pl.ds(pl.multiple_of(g * group + side * part[0], part[0]), part[0])
+
+    def share_early(g):
+        for s in split[1:]:
+            for mask in wide_masks:
+                if (g, s, mask) in early:
+                    early[g, s, mask].wait_recv()
+        if late > 1:
+            place = factors.at[core_rows(g), pl.ds(rank, (late - 1) * rank)]
+            core_move[g, 0] = remote(place, place, 1)
+
+    def share_late(g):
+        for mask in wide_masks:
+            late_move[g, mask].wait_recv()
+        place = factors.at[core_rows(g), pl.ds(late * rank, rows[late])]
+        core_move[g, 1] = remote(place, place, 1)
+
+    def end_group(g):
+        early[g, 0, 1].wait_recv()
+        if late > 1:
+            core_move[g, 0].wait_recv()
+        core_move[g, 1].wait_recv()
+        finish(g)
 
     def finish(g):
         lanes = slice(g * group, (g + 1) * group)
@@ -349,7 +389,7 @@
         mine = pl.ds(g * group, group)
         finals.append(local(est_v.at[:, mine], out.at[:, mine], 8 + g))
 
-    last = 1 + levels + len(split)
+    last = 3 + levels
     for wave in range(last + groups - 1):
         for g in reversed(range(groups)):
             step = wave - g
@@ -368,12 +408,32 @@
                 up(g, step - 1)
                 if g == 0 and step < levels:
                     share_gram(step)
+                if step == levels:
+                    share_early(g)
+            elif step == levels + 1:
+                share_late(g)
             else:
-                down(g, step - 1 - levels)
+                end_group(g)
 
     for copy in sent:
         copy.wait_send()
     for copy in finals:
+        copy.wait()
+
+
+def move_kernel(pieces, source, out, held, in_sem, out_sem):
+    step = source.shape[0] // pieces
+    places = [pl.ds(i * step, step) for i in range(pieces)]
+    arrive = [
+        pltpu.make_async_copy(source.at[p], held.at[p], in_sem.at[i]) for i, p in enumerate(places)
+    ]
+    leave = [pltpu.make_async_copy(held.at[p], out.at[p], out_sem.at[i]) for i, p in enumerate(places)]
+    for copy in arrive:
+        copy.start()
+    for first, second in zip(arrive, leave):
+        first.wait()
+        second.start()
+    for copy in leave:
         copy.wait()
 
 
@@ -408,6 +468,8 @@
         vm((leaf, wide), BF),
         vm((leaf, trend_rank), BF),
         vm((leaf, leaf), BF),
+        vm((leaf, 128), F32),
+        vm((leaf, group), BF),
         vm((leaf, cols), F32),
         vm((cols, leaf), BF),
         vm((levels + 1,) + coupling.shape, BF),
@@ -421,12 +483,15 @@
     scratch += [vm((part[s], rank), BF) for s in every] * groups
     scratch += [vm((2, rank, rows[s + 1]), BF) for s in every]
     scratch += [vm((rank // 2, width[s + 1]), BF) for s in range(levels - 1)] * 2
+    late = sum(held[s] != part[s] for s in every)
+    reach = (1 << late >> 1) - 1
+    copies = 6 * levels + groups * (levels + 2 * reach + reach + 3)
     scratch += [
         pltpu.SemaphoreType.DMA((8 + groups,)),
-        pltpu.SemaphoreType.DMA((6 + 3 * groups, levels)),
-        pltpu.SemaphoreType.DMA((6 + 3 * groups, levels)),
+        pltpu.SemaphoreType.DMA((copies,)),
+        pltpu.SemaphoreType.DMA((copies,)),
     ]
-    return pl.pallas_call(
+    swept = pl.pallas_call(
         functools.partial(sweep_kernel, bits_inner, levels, rank, group, tile),
         out_shape=jax.ShapeDtypeStruct((leaf, cols), F32),
         in_specs=[pl.BlockSpec(memory_space=pltpu.HBM)] * 8,
@@ -446,6 +511,20 @@
         trend_basis,
         trend_correct,
     )
+    pieces = 8 if leaf % 64 == 0 else 1
+    return pl.pallas_call(
+        functools.partial(move_kernel, pieces),
+        out_shape=jax.ShapeDtypeStruct((leaf, cols), F32),
+        in_specs=[pl.BlockSpec(memory_space=pl.ANY)],
+        out_specs=pl.BlockSpec(memory_space=pl.ANY),
+        scratch_shapes=[
+            vm((leaf, cols), F32),
+            pltpu.SemaphoreType.DMA((pieces,)),
+            pltpu.SemaphoreType.DMA((pieces,)),
+        ],
+        compiler_params=pltpu.CompilerParams(vmem_limit_bytes=62 * 1024 * 1024),
+        name="move_result",
+    )(swept)
 
 
 def solution(mesh):

time: 51.8 us -> 49 us (0.946)
  local copies, waits for them, and re-layouts: 3.76 us -> 0 us
  Pallas kernels: 47.9 us -> 48.7 us
    unnamed x1 -> x0, local copies, waits for them, and re-layouts: 3.76 us -> none
    pallas_call x0 -> x1, Pallas kernels: none -> 2.79 us  [body(): pl.pallas_call(functools.partial(move_kernel, pieces), out_shape=jax.Shap...]
    pallas_call x1, Pallas kernels: 47.9 us -> 45.9 us  [body(): pl.pallas_call(functools.partial(sweep_kernel, bits_inner, levels, rank,...]
where the time goes in v4:
time: 49 us; the launch traced here: 48.7 us
  Pallas kernels  48.7 us (99%)
    pallas_call x1, Pallas kernels, body(): pl.pallas_call(functools.partial(sweep_kernel, bits_inner, levels, rank,...  45.9 us
    pallas_call x1, Pallas kernels, body(): pl.pallas_call(functools.partial(move_kernel, pieces), out_shape=jax.Shap...  2.79 us

profile of v4, /device:TPU:1, one launch (start us, length us, event | category | flops | bytes accessed | tf_op | source)
XLA Modules:
  0.0 48.7 jit_solution(4543986473399725457)
XLA Ops:
  0.0 45.9 %tree_sweep.1.source = f32[1024,768]{1,0:T(8,128)} custom-call(f32[1024,768]{1,0:T(8,128)} %observed.1, s32[1,1024]{1,0:T(1,128)} %order.1, bf16[1024,1024]{1,0:T(8,128)(2,1)} %inverse.1, bf16[1024,640]{1,0:T(8,128)(2,1)} %project.1, bf16[1024,640]{1,0:T(8,128)(2,1)} %correct.1, bf16[256,256]{1,0:T(8,128)(2,1)} %coupling.1, bf16[1024,256]{1,0:T(8,128)(2,1)} %trend.1, ...), custom_call_target="tpu_custom_call" | custom-call | tf_op jit(solution)/shard_map/tree_sweep/pallas_call | solution.py:494
  46.0 2.8 %move_result.1 = f32[1024,768]{1,0:T(8,128)} custom-call(f32[1024,768]{1,0:T(8,128)} %tree_sweep.1.source), custom_call_target="tpu_custom_call" | custom-call | tf_op jit(solution)/shard_map/move_result/pallas_call | solution.py:515

commit v5 on v4

--- a/solution.py
+++ b/solution.py
@@ -312,15 +312,14 @@
         own_head, other_head = own[:, :rank], other[:, :rank]
         one = jnp.where(first_side, own_head, other_head).astype(BF)
         two = jnp.where(first_side, other_head, own_head).astype(BF)
-        block = blocks[block_of[s]]
-        factor = dot_nt(one, block[:, :rank]) + dot_nt(two, block[:, rank:])
+        stacked = jnp.concatenate([one, two], 1)
+        factor = dot_nt(stacked, blocks[block_of[s]])
         mine = jnp.where(first_side, factor[:, :rank], factor[:, rank:]).astype(BF)
         theirs = jnp.where(first_side, factor[:, rank:], factor[:, :rank]).astype(BF)
         new = (
             own[:, rank:]
             + other[:, rank:]
-            - dot(mine, gram[s][0])
-            - dot(theirs, gram[s][1])
+            - dot(jnp.concatenate([mine, theirs], 1), gram[s][...].reshape(2 * rank, rows[s + 1]))
         )
         sums[g][s + 1][...] = new
         if s + 1 < levels:

time: 49 us -> 48.7 us (level)
  no operation moved by 1% of the time
where the time goes in v5:
time: 48.7 us; the launch traced here: 48.5 us
  Pallas kernels  48.5 us (100%)
    pallas_call x1, Pallas kernels, body(): pl.pallas_call(functools.partial(sweep_kernel, bits_inner, levels, rank,...  45.7 us
    pallas_call x1, Pallas kernels, body(): pl.pallas_call(functools.partial(move_kernel, pieces), out_shape=jax.Shap...  2.79 us

profile of v5, /device:TPU:1, one launch (start us, length us, event | category | flops | bytes accessed | tf_op | source)
XLA Modules:
  0.0 48.5 jit_solution(8270198259369368142)
XLA Ops:
  0.0 45.7 %tree_sweep.1.source = f32[1024,768]{1,0:T(8,128)} custom-call(f32[1024,768]{1,0:T(8,128)} %observed.1, s32[1,1024]{1,0:T(1,128)} %order.1, bf16[1024,1024]{1,0:T(8,128)(2,1)} %inverse.1, bf16[1024,640]{1,0:T(8,128)(2,1)} %project.1, bf16[1024,640]{1,0:T(8,128)(2,1)} %correct.1, bf16[256,256]{1,0:T(8,128)(2,1)} %coupling.1, bf16[1024,256]{1,0:T(8,128)(2,1)} %trend.1, ...), custom_call_target="tpu_custom_call" | custom-call | tf_op jit(solution)/shard_map/tree_sweep/pallas_call | solution.py:493
  45.7 2.8 %move_result.1 = f32[1024,768]{1,0:T(8,128)} custom-call(f32[1024,768]{1,0:T(8,128)} %tree_sweep.1.source), custom_call_target="tpu_custom_call" | custom-call | tf_op jit(solution)/shard_map/move_result/pallas_call | solution.py:514

commit v6 on v5

--- a/solution.py
+++ b/solution.py
@@ -397,15 +397,13 @@
             if step == 0:
                 start_group(g)
             elif step <= levels:
-                if g == 0:
+                if g == 0 and step == 1:
+                    share_gram(0)
+                up(g, step - 1)
+                if g == 0 and step < levels:
                     if step + 1 < levels:
                         advance_block(step + 1)
-                    if step < levels:
-                        advance_gram(step)
-                    if step == 1:
-                        share_gram(0)
-                up(g, step - 1)
-                if g == 0 and step < levels:
+                    advance_gram(step)
                     share_gram(step)
                 if step == levels:
                     share_early(g)

time: 48.7 us -> 48.8 us (level)
  no operation moved by 1% of the time
where the time goes in v6:
time: 48.8 us; the launch traced here: 48.5 us
  Pallas kernels  48.5 us (99%)
    pallas_call x1, Pallas kernels, body(): pl.pallas_call(functools.partial(sweep_kernel, bits_inner, levels, rank,...  45.7 us
    pallas_call x1, Pallas kernels, body(): pl.pallas_call(functools.partial(move_kernel, pieces), out_shape=jax.Shap...  2.79 us

profile of v6, /device:TPU:1, one launch (start us, length us, event | category | flops | bytes accessed | tf_op | source)
XLA Modules:
  0.0 48.5 jit_solution(16690779123447808761)
XLA Ops:
  0.0 45.7 %tree_sweep.1.source = f32[1024,768]{1,0:T(8,128)} custom-call(f32[1024,768]{1,0:T(8,128)} %observed.1, s32[1,1024]{1,0:T(1,128)} %order.1, bf16[1024,1024]{1,0:T(8,128)(2,1)} %inverse.1, bf16[1024,640]{1,0:T(8,128)(2,1)} %project.1, bf16[1024,640]{1,0:T(8,128)(2,1)} %correct.1, bf16[256,256]{1,0:T(8,128)(2,1)} %coupling.1, bf16[1024,256]{1,0:T(8,128)(2,1)} %trend.1, ...), custom_call_target="tpu_custom_call" | custom-call | tf_op jit(solution)/shard_map/tree_sweep/pallas_call | solution.py:491
  45.8 2.8 %move_result.1 = f32[1024,768]{1,0:T(8,128)} custom-call(f32[1024,768]{1,0:T(8,128)} %tree_sweep.1.source), custom_call_target="tpu_custom_call" | custom-call | tf_op jit(solution)/shard_map/move_result/pallas_call | solution.py:512

commit v7 on v6

--- a/solution.py
+++ b/solution.py
@@ -390,7 +390,7 @@
 
     last = 3 + levels
     for wave in range(last + groups - 1):
-        for g in reversed(range(groups)):
+        for g in range(groups):
             step = wave - g
             if step < 0 or step >= last:
                 continue

time: 48.8 us -> 51.6 us (1.057)
  Pallas kernels: 48.5 us -> 51.5 us
    pallas_call x1, Pallas kernels: 45.7 us -> 48.7 us  [body(): pl.pallas_call(functools.partial(sweep_kernel, bits_inner, levels, rank,...]
where the time goes in v7:
time: 51.6 us; the launch traced here: 51.5 us
  Pallas kernels  51.5 us (100%)
    pallas_call x1, Pallas kernels, body(): pl.pallas_call(functools.partial(sweep_kernel, bits_inner, levels, rank,...  48.7 us
    pallas_call x1, Pallas kernels, body(): pl.pallas_call(functools.partial(move_kernel, pieces), out_shape=jax.Shap...  2.79 us

profile of v7, /device:TPU:1, one launch (start us, length us, event | category | flops | bytes accessed | tf_op | source)
XLA Modules:
  0.0 51.5 jit_solution(8099465767642352689)
XLA Ops:
  0.0 48.7 %tree_sweep.1.source = f32[1024,768]{1,0:T(8,128)} custom-call(f32[1024,768]{1,0:T(8,128)} %observed.1, s32[1,1024]{1,0:T(1,128)} %order.1, bf16[1024,1024]{1,0:T(8,128)(2,1)} %inverse.1, bf16[1024,640]{1,0:T(8,128)(2,1)} %project.1, bf16[1024,640]{1,0:T(8,128)(2,1)} %correct.1, bf16[256,256]{1,0:T(8,128)(2,1)} %coupling.1, bf16[1024,256]{1,0:T(8,128)(2,1)} %trend.1, ...), custom_call_target="tpu_custom_call" | custom-call | tf_op jit(solution)/shard_map/tree_sweep/pallas_call | solution.py:491
  48.7 2.8 %move_result.1 = f32[1024,768]{1,0:T(8,128)} custom-call(f32[1024,768]{1,0:T(8,128)} %tree_sweep.1.source), custom_call_target="tpu_custom_call" | custom-call | tf_op jit(solution)/shard_map/move_result/pallas_call | solution.py:512
